TPU v7x, 32 devices: a whole 2x2x4 slice. The times are simulated.
32 devices in a mesh: group: 2 (over y), row: 4 (over z), col: 4 (over x, core).
Axes of the slice: x: 2, y: 2, z: 4, core: 2. Of those that a mesh axis runs over, the one named last changes fastest.
Arguments:
- features: bfloat16 [65536, 128], P(('group', 'row', 'col')), parts along dimension 0, may hold values from -6 to 6
- cotangent: bfloat16 [65536, 128], P(('group', 'row', 'col')), parts along dimension 0, may hold values from -6 to 6
- fine_weight: bfloat16 [128, 128], replicated, may hold values from -0.5 to 0.5
- middle_weight: bfloat16 [128, 128], replicated, may hold values from -0.5 to 0.5
- top_weight: bfloat16 [128, 128], replicated, may hold values from -0.5 to 0.5
- tile_bank: bfloat16 [32, 128, 128], replicated, may hold values from -0.25 to 0.25
- fine_source: int32 [4096], P(('group', 'row', 'col')), parts along dimension 0, may hold values from 0 to 23
- fine_target: int32 [4096], P(('group', 'row', 'col')), parts along dimension 0, may hold values from 0 to 15
- fine_kind: int32 [4096], P(('group', 'row', 'col')), parts along dimension 0, may hold values from 0 to 31
- tile_count: int32 [32], P(('group', 'row', 'col')), parts along dimension 0, may hold values from 25 to 128, as said below
- fine_sends: int32 [256], P(('group', 'row', 'col')), parts along dimension 0, may hold values from 0 to 15
- fine_pool: int32 [65536], P(('group', 'row', 'col')), parts along dimension 0, may hold values from 0 to 1023
- middle_source: int32 [256], P(('group', 'row')), parts along dimension 0, may hold values from 0 to 11
- middle_target: int32 [256], P(('group', 'row')), parts along dimension 0, may hold values from 0 to 7
- middle_kind: int32 [256], P(('group', 'row')), parts along dimension 0, may hold values from 0 to 31
- middle_sends: int32 [32], P(('group', 'row')), parts along dimension 0, may hold values from 0 to 7
- middle_pool: int32 [8192], P(('group', 'row')), parts along dimension 0, may hold values from 0 to 511
- top_source: int32 [32], P('group'), parts along dimension 0, may hold values from 0 to 3
- top_kind: int32 [32], P('group'), parts along dimension 0, may hold values from 0 to 31
Outputs:
- fine_out: bfloat16 [65536, 128], P(('group', 'row', 'col')), parts along dimension 0
- grad_features: bfloat16 [65536, 128], P(('group', 'row', 'col')), parts along dimension 0
- weight_grads: float32 [6, 128, 128], P('group'), parts along dimension 0
There are 2 independent parts, one for each index of `group`. A program takes and returns all parts, laid end to end along the dimension named above; an argument that names none is the same for every part. Nothing has to cross between parts.
Inputs may be any that keep to these rules, and one draw needn't show every extreme that they name: Only the first tile_count[p] tile slots of partition p are live; later slots are ignored.
All inputs are finite; a program needn't handle non-finite values.
Results may differ from a plain program's by a relative error of at most 0.028.
Values may be sent and summed in bfloat16 or wider, within the bound.
A program may use at most 64 MiB of HBM per device.

v0:
```python
import math

import jax
import jax.numpy as jnp
from jax import lax
from jax.sharding import PartitionSpec as P

tile_group = 8


def extended_2(cells, sides, width):
    for axis, dim in sides:
        count = lax.axis_size(axis)
        ends = count - 1
        head = lax.slice_in_dim(cells, 0, width, axis=dim)
        tail = lax.slice_in_dim(cells, cells.shape[dim] - width, cells.shape[dim], axis=dim)
        cells = jnp.concatenate(
            [
                lax.ppermute(tail, axis, [(i, (i + 1) % count) for i in range(ends)]),
                cells,
                lax.ppermute(head, axis, [((i + 1) % count, i) for i in range(ends)]),
            ],
            axis=dim,
        )
    return cells


def gelu_slope(value):
    return jax.vjp(jax.nn.gelu, value)[1](jnp.ones_like(value))[0]


def one_hot_rows(index, extent, dtype):
    return (index[:, None] == jnp.arange(extent, dtype=jnp.int32)[None, :]).astype(dtype)


def pool_rows(values, index, segments):
    rows = values.shape[0]
    step = math.gcd(rows, 128)
    value_blocks = values.reshape(rows // step, step, values.shape[1])
    index_blocks = index.reshape(rows // step, step)

    def add_block(total, pair):
        block_values, block_index = pair
        table = one_hot_rows(block_index, segments, jnp.float32)
        return (total + jnp.dot(table.T, block_values, precision=lax.Precision.HIGHEST), None)

    initial = jnp.zeros((segments, values.shape[1]), jnp.float32)
    total, unused = lax.scan(add_block, initial, (value_blocks, index_blocks))
    return total


def pick_rows(table, index):
    rows = index.shape[0]
    step = math.gcd(rows, 128)
    index_blocks = index.reshape(rows // step, step)

    def take_block(block_index):
        selector = one_hot_rows(block_index, table.shape[0], jnp.float32)
        return jnp.dot(selector, table, precision=lax.Precision.HIGHEST)

    return lax.map(take_block, index_blocks).reshape(rows, table.shape[1])


def select_blocks(stack, index):
    selector = one_hot_rows(index, stack.shape[0], stack.dtype)
    return jnp.einsum("ts,sjh->tjh", selector, stack, preferred_element_type=jnp.float32).astype(
        stack.dtype
    )


def add_blocks(products, index, extent):
    selector = one_hot_rows(index, extent, jnp.float32)
    return jnp.einsum("tb,tih->bih", selector, products, precision=lax.Precision.HIGHEST)


def tile_forward(bank, kinds, sources, targets, live, extended, blocks):
    count = kinds.shape[0]
    group = min(tile_group, count)

    def add_group(total, index):
        start = index * group
        kind_part = lax.dynamic_slice_in_dim(kinds, start, group)
        source_part = lax.dynamic_slice_in_dim(sources, start, group)
        target_part = lax.dynamic_slice_in_dim(targets, start, group)
        live_part = lax.dynamic_slice_in_dim(live, start, group)
        tiles = select_blocks(bank, kind_part)
        inputs = select_blocks(extended, source_part)
        products = jnp.einsum("tij,tjh->tih", tiles, inputs, preferred_element_type=jnp.float32)
        products = products * live_part.astype(jnp.float32)[:, None, None]
        return (total + add_blocks(products, target_part, blocks), None)

    initial = jnp.zeros((blocks,) + extended.shape[1:], jnp.float32)
    total, unused = lax.scan(add_group, initial, jnp.arange(count // group, dtype=jnp.int32))
    return total


def tile_backward(bank, kinds, sources, targets, live, grads, extent):
    count = kinds.shape[0]
    group = min(tile_group, count)

    def add_group(total, index):
        start = index * group
        kind_part = lax.dynamic_slice_in_dim(kinds, start, group)
        source_part = lax.dynamic_slice_in_dim(sources, start, group)
        target_part = lax.dynamic_slice_in_dim(targets, start, group)
        live_part = lax.dynamic_slice_in_dim(live, start, group)
        tiles = select_blocks(bank, kind_part)
        inputs = select_blocks(grads, target_part)
        products = jnp.einsum("tji,tjh->tih", tiles, inputs, preferred_element_type=jnp.float32)
        products = products * live_part.astype(jnp.float32)[:, None, None]
        return (total + add_blocks(products, source_part, extent), None)

    initial = jnp.zeros((extent,) + grads.shape[1:], jnp.float32)
    total, unused = lax.scan(add_group, initial, jnp.arange(count // group, dtype=jnp.int32))
    return total


def local(
    features,
    cotangent,
    fine_weight,
    middle_weight,
    top_weight,
    tile_bank,
    fine_source,
    fine_target,
    fine_kind,
    tile_count,
    fine_sends,
    fine_pool,
    middle_source,
    middle_target,
    middle_kind,
    middle_sends,
    middle_pool,
    top_source,
    top_kind,
):
    row_count = lax.axis_size("row")
    column_count = lax.axis_size("col")
    row_index = lax.axis_index("row")
    column_index = lax.axis_index("col")
    block_rows = tile_bank.shape[1]
    width = features.shape[1]
    own_rows = features.shape[0]
    own_blocks = own_rows // block_rows
    send_count = fine_sends.shape[0] // 4
    halo_rows = send_count * block_rows
    middle_rows = middle_pool.shape[0]
    middle_blocks = middle_rows // block_rows
    middle_send = middle_sends.shape[0] // 2
    middle_halo = middle_send * block_rows
    top_rows = block_rows * column_count
    top_slots = top_source.shape[0] // column_count
    pool_two = (middle_rows / (own_rows * column_count)) ** 0.5
    pool_three = (top_rows / (middle_rows * row_count)) ** 0.5
    fine_message = jnp.dot(features, fine_weight, preferred_element_type=jnp.float32).astype(
        jnp.bfloat16
    )
    fine_blocks = fine_message.reshape(own_blocks, block_rows, width)
    outgoing = fine_blocks[fine_sends].reshape(4, halo_rows, width)
    vertical = extended_2(jnp.concatenate([outgoing[1], outgoing[0]], 0), (("row", 0),), halo_rows)
    sideways = extended_2(jnp.concatenate([outgoing[3], outgoing[2]], 0), (("col", 0),), halo_rows)
    received = jnp.concatenate(
        [vertical[:halo_rows], vertical[-halo_rows:], sideways[:halo_rows], sideways[-halo_rows:]],
        0,
    )
    fine_extended = jnp.concatenate(
        [fine_blocks, received.reshape(4 * send_count, block_rows, width)], 0
    )
    live_fine = jnp.arange(fine_source.shape[0], dtype=jnp.int32) < tile_count[0]
    fine_summed = tile_forward(
        tile_bank, fine_kind, fine_source, fine_target, live_fine, fine_extended, own_blocks
    ).reshape(own_rows, width)
    fine_hidden = features.astype(jnp.float32) + jax.nn.gelu(fine_summed)
    grad_out = cotangent.astype(jnp.float32)
    pooled = pool_rows(fine_hidden, fine_pool, middle_rows)
    grad_pooled = pool_rows(grad_out, fine_pool, middle_rows)
    pooled_total, grad_pooled_total = (
        lax.psum(pooled.astype(jnp.bfloat16), "col").astype(jnp.float32),
        lax.psum(grad_pooled.astype(jnp.bfloat16), "col").astype(jnp.float32),
    )
    coarse = pooled_total * pool_two
    grad_middle_sum = grad_pooled_total * pool_two
    coarse_low = coarse.astype(jnp.bfloat16)
    middle_message = jnp.dot(coarse_low, middle_weight, preferred_element_type=jnp.float32).astype(
        jnp.bfloat16
    )
    middle_stack = middle_message.reshape(middle_blocks, block_rows, width)
    middle_out = middle_stack[middle_sends].reshape(2, middle_halo, width)
    middle_vertical = extended_2(
        jnp.concatenate([middle_out[1], middle_out[0]], 0), (("row", 0),), middle_halo
    )
    middle_received = jnp.concatenate(
        [middle_vertical[:middle_halo], middle_vertical[-middle_halo:]], 0
    )
    middle_extended = jnp.concatenate(
        [middle_stack, middle_received.reshape(2 * middle_send, block_rows, width)], 0
    )
    live_middle = jnp.ones(middle_source.shape, bool)
    middle_summed = tile_forward(
        tile_bank,
        middle_kind,
        middle_source,
        middle_target,
        live_middle,
        middle_extended,
        middle_blocks,
    ).reshape(middle_rows, width)
    middle_hidden = coarse + jax.nn.gelu(middle_summed)
    local_ids = middle_pool - column_index * block_rows
    partial_top = pool_rows(middle_hidden, local_ids, block_rows)
    partial_grad = pool_rows(grad_middle_sum, local_ids, block_rows)
    top_total, grad_total = (
        lax.psum(partial_top.astype(jnp.bfloat16), "row").astype(jnp.float32),
        lax.psum(partial_grad.astype(jnp.bfloat16), "row").astype(jnp.float32),
    )
    top_state = top_total * pool_three
    grad_top_state = grad_total * pool_three
    top_low = top_state.astype(jnp.bfloat16)
    top_message = jnp.dot(top_low, top_weight, preferred_element_type=jnp.float32).astype(
        jnp.bfloat16
    )
    all_messages = lax.all_gather(top_message, "col", axis=0, tiled=True)
    my_sources = lax.dynamic_slice_in_dim(top_source, column_index * top_slots, top_slots)
    my_kinds = lax.dynamic_slice_in_dim(top_kind, column_index * top_slots, top_slots)
    zero_targets = jnp.zeros((top_slots,), jnp.int32)
    live_own = jnp.ones((top_slots,), bool)
    top_summed = tile_forward(
        tile_bank,
        my_kinds,
        my_sources,
        zero_targets,
        live_own,
        all_messages.reshape(column_count, block_rows, width),
        1,
    ).reshape(block_rows, width)
    top_hidden = top_state + jax.nn.gelu(top_summed)
    top_full = lax.all_gather(top_hidden.astype(jnp.bfloat16), "col", axis=0, tiled=True).astype(
        top_hidden.dtype
    )
    middle_unpooled = middle_hidden + pool_three * pick_rows(top_full, middle_pool)
    grad_top_summed = (grad_top_state * gelu_slope(top_summed)).astype(jnp.bfloat16)
    back_terms = tile_backward(
        tile_bank,
        my_kinds,
        my_sources,
        zero_targets,
        live_own,
        grad_top_summed.reshape(1, block_rows, width),
        column_count,
    ).reshape(top_rows, width)
    grad_top_message = lax.psum_scatter(
        back_terms.astype(jnp.bfloat16), "col", scatter_dimension=0, tiled=True
    )
    share = block_rows // row_count
    top_slice = lax.dynamic_slice_in_dim(top_low, row_index * share, share)
    grad_slice = lax.dynamic_slice_in_dim(grad_top_message, row_index * share, share)
    top_grad = jnp.dot(top_slice.T, grad_slice, preferred_element_type=jnp.float32)
    grad_top_own = grad_top_state + jnp.dot(
        grad_top_message, top_weight.T, preferred_element_type=jnp.float32
    )
    grad_top_full = lax.all_gather(
        grad_top_own.astype(jnp.bfloat16), "col", axis=0, tiled=True
    ).astype(grad_top_own.dtype)
    fine_out = (fine_hidden + pool_two * pick_rows(middle_unpooled, fine_pool)).astype(jnp.bfloat16)
    grad_middle_hidden = grad_middle_sum + pool_three * pick_rows(grad_top_full, middle_pool)
    grad_middle_summed = (grad_middle_hidden * gelu_slope(middle_summed)).astype(jnp.bfloat16)
    middle_terms = tile_backward(
        tile_bank,
        middle_kind,
        middle_source,
        middle_target,
        live_middle,
        grad_middle_summed.reshape(middle_blocks, block_rows, width),
        middle_blocks + 2 * middle_send,
    )
    middle_back = middle_terms[middle_blocks:].reshape(2 * middle_halo, width)
    middle_returned = extended_2(
        middle_back.astype(jnp.bfloat16), (("row", 0),), middle_halo
    ).astype(middle_back.dtype)
    middle_home = jnp.concatenate(
        [middle_returned[-middle_halo:], middle_returned[:middle_halo]], 0
    )
    grad_middle_message = middle_terms[:middle_blocks] + add_blocks(
        middle_home.reshape(2 * middle_send, block_rows, width), middle_sends, middle_blocks
    )
    grad_middle_message = grad_middle_message.reshape(middle_rows, width).astype(jnp.bfloat16)
    middle_share = middle_rows // column_count
    coarse_slice = lax.dynamic_slice_in_dim(coarse_low, column_index * middle_share, middle_share)
    message_slice = lax.dynamic_slice_in_dim(
        grad_middle_message, column_index * middle_share, middle_share
    )
    middle_grad = jnp.dot(coarse_slice.T, message_slice, preferred_element_type=jnp.float32)
    grad_coarse = grad_middle_hidden + jnp.dot(
        grad_middle_message, middle_weight.T, preferred_element_type=jnp.float32
    )
    grad_fine_hidden = grad_out + pool_two * pick_rows(grad_coarse, fine_pool)
    grad_fine_summed = (grad_fine_hidden * gelu_slope(fine_summed)).astype(jnp.bfloat16)
    fine_terms = tile_backward(
        tile_bank,
        fine_kind,
        fine_source,
        fine_target,
        live_fine,
        grad_fine_summed.reshape(own_blocks, block_rows, width),
        own_blocks + 4 * send_count,
    )
    back_vertical = fine_terms[own_blocks : own_blocks + 2 * send_count].reshape(
        2 * halo_rows, width
    )
    back_sideways = fine_terms[own_blocks + 2 * send_count :].reshape(2 * halo_rows, width)
    rows_home = extended_2(back_vertical.astype(jnp.bfloat16), (("row", 0),), halo_rows).astype(
        back_vertical.dtype
    )
    columns_home = extended_2(back_sideways.astype(jnp.bfloat16), (("col", 0),), halo_rows).astype(
        back_sideways.dtype
    )
    fine_home = jnp.concatenate(
        [
            rows_home[-halo_rows:],
            rows_home[:halo_rows],
            columns_home[-halo_rows:],
            columns_home[:halo_rows],
        ],
        0,
    )
    grad_fine_message = fine_terms[:own_blocks] + add_blocks(
        fine_home.reshape(4 * send_count, block_rows, width), fine_sends, own_blocks
    )
    grad_fine_message = grad_fine_message.reshape(own_rows, width).astype(jnp.bfloat16)
    fine_grad = jnp.dot(features.T, grad_fine_message, preferred_element_type=jnp.float32)
    grad_features = (
        grad_fine_hidden
        + jnp.dot(grad_fine_message, fine_weight.T, preferred_element_type=jnp.float32)
    ).astype(jnp.bfloat16)
    totals = lax.psum(jnp.stack([fine_grad, middle_grad, top_grad]), ("row", "col"))
    fine_total = own_rows * row_count * column_count
    middle_total = middle_rows * row_count
    scales = jnp.array(
        [fine_total ** (-0.5), middle_total ** (-0.5), top_rows ** (-0.5)], jnp.float32
    )
    return (fine_out, grad_features, totals * scales[:, None, None])


def solution(mesh):
    in_specs = (
        P(("group", "row", "col"), None),
        P(("group", "row", "col"), None),
        P(),
        P(),
        P(),
        P(),
        P(("group", "row", "col")),
        P(("group", "row", "col")),
        P(("group", "row", "col")),
        P(("group", "row", "col")),
        P(("group", "row", "col")),
        P(("group", "row", "col")),
        P(("group", "row")),
        P(("group", "row")),
        P(("group", "row")),
        P(("group", "row")),
        P(("group", "row")),
        P("group"),
        P("group"),
    )
    out_specs = (
        P(("group", "row", "col"), None),
        P(("group", "row", "col"), None),
        P("group", None, None),
    )
    return jax.shard_map(local, mesh=mesh, in_specs=in_specs, out_specs=out_specs, check_vma=False)
```

profile of v0, /device:TPU:0, one launch (start us, length us, event | category | flops | bytes accessed | tf_op | source)
XLA Modules:
  0.0 598.9 jit_solution(9251472735978767195)
XLA Ops:
  11.8 3.0 collective-permute-start.2
  16.2 6.2 %collective-permute-start = (bf16[256,128]{1,0:T(8,128)(2,1)S(1)}, bf16[256,128]{1,0:T(8,128)(2,1)}, u32[]{:S(2)}, u32[]{:S(2)}) collective-permute-start(bf16[256,128]{1,0:T(8,128)(2,1)S(1)} %bitcast.307), channel_id=1, source_target_pairs={{0,4},{4,8},{8,12},{1,5},{5,9},{9,13},{2,6},{6,10},{10,14},{3,7},{... | collective-permute-start | bytes 196616 | tf_op jit(solution)/shard_map/ppermute | solution.py:19
  24.1 38.0 %while.144 = (s32[]{:T(128)}, f32[1024,128]{1,0:T(8,128)S(1)}, s32[16,128]{1,0:T(8,128)}, f32[16,128,128]{2,1,0:T(8,128)}, s32[]{:T(128)}, /*index=5*/s32[]{:T(128)}) while((s32[]{:T(128)}, f32[1024,128]{1,0:T(8,128)S(1)}, s32[16,128]{1,0:T(8,128)}, f32[16,128,128]{2,1,0:T(8,128)}, s32[]{:T(128)}, /*index=5*/s32[]{:T(128)}) %tuple.280), condition=%wide.region_15.16_spmd.clone, body=%wide.region_14.15_spmd.clone.sunk | while | flops 201719808 | bytes 1115743 | solution.py:48
  64.0 69.1 %while.140 = (s32[]{:T(128)}, f32[16,128,128]{2,0,1:T(8,128)S(1)}, s32[16]{0:T(128)S(1)}, s32[128]{0:T(128)S(1)}, s32[128]{0:T(128)S(1)}, /*index=5*/bf16[32,128...) while((s32[]{:T(128)}, f32[16,128,128]{2,0,1:T(8,128)S(1)}, ...), condition=%wide.region_1.2_spmd.clone, body=%wide.region_0.1_spmd.clone.sunk | while | flops 74056272 | bytes 6029889 | solution.py:93
  135.5 23.7 %while.141 = (s32[]{:T(128)}, f32[1024,128]{1,0:T(8,128)S(1)}, s32[16,128]{1,0:T(8,128)}, f32[16,128,128]{2,1,0:T(8,128)S(1)}, s32[]{:T(128)}, /*index=5*/s32[]{:T(128)}) while((s32[]{:T(128)}, f32[1024,128]{1,0:T(8,128)S(1)}, s32[16,128]{1,0:T(8,128)}, f32[16,128,128]{2,1,0:T(8,128)S(1)}, s32[]{:T(128)}, ...), condition=%wide.region_3.4_spmd.clone, body=%wide.region_2.3_spmd.clone.sunk | while | flops 201719808 | bytes 1115743 | solution.py:48
  160.1 34.0 %all-reduce.8.cloned.1.call-done = (bf16[1024,128]{1,0:T(8,128)(2,1)}, bf16[1024,128]{1,0:T(8,128)(2,1)}) async-done(((bf16[1024,128]{1,0:T(8,128)(2,1)}, bf16[1024,128]{1,0:T(8,128)(2,1)}), (bf16[1024,128]{1,0:T(8,128)(2,1)}, bf16[1024,128]{1,0:T(8,128)(2,1)})) %all-reduce.8.cloned.1.call-update) | async-done | bytes 524304 | tf_op jit(solution)/shard_map/psum | solution.py:180
  197.1 4.5 collective-permute-start.4
  203.7 13.9 %while.142 = (s32[]{:T(128)}, f32[8,128,128]{2,0,1:T(8,128)S(1)}, s32[4]{0:T(128)S(1)}, s32[32]{0:T(128)S(1)}, s32[32]{0:T(128)S(1)}, /*index=5*/bf16[32,128,128...) while((s32[]{:T(128)}, f32[8,128,128]{2,0,1:T(8,128)S(1)}, ...), condition=%wide.region_6.7_spmd.clone, body=%wide.region_5.6_spmd.clone.sunk | while | flops 57934244 | bytes 4588013 | solution.py:93
  219.5 3.0 while.143
  223.1 3.0 while.145
  227.7 34.3 %all-reduce.10.cloned.1.call-done = (bf16[128,128]{1,0:T(8,128)(2,1)}, bf16[128,128]{1,0:T(8,128)(2,1)}) async-done(((bf16[128,128]{1,0:T(8,128)(2,1)}, bf16[128,128]{1,0:T(8,128)(2,1)}), (bf16[128,128]{1,0:T(8,128)(2,1)}, bf16[128,128]{1,0:T(8,128)(2,1)})) %all-reduce.10.cloned.1.call-update) | async-done | bytes 65552 | tf_op jit(solution)/shard_map/psum | solution.py:215
  262.9 5.4 all_gather.9
  270.9 5.6 all_gather.10
  276.6 2.8 while.136
  281.6 28.3 %while.137 = (s32[]{:T(128)}, f32[16,128,128]{2,1,0:T(8,128)}, s32[16,128]{1,0:T(8,128)}, f32[1024,128]{1,0:T(8,128)S(1)}, s32[]{:T(128)}) while((s32[]{:T(128)}, f32[16,128,128]{2,1,0:T(8,128)}, s32[16,128]{1,0:T(8,128)}, f32[1024,128]{1,0:T(8,128)S(1)}, s32[]{:T(128)}) %tuple.282), condition=%wide.region_13.14_spmd, body=%wide.region_12.13_spmd.sunk | while | flops 201457664 | bytes 591437 | solution.py:61
  311.4 2.3 broadcast_multiply_fusion.1
  313.7 17.1 %reduce-scatter.2.cloned.1.call-done = bf16[128,128]{1,0:T(8,128)(2,1)} async-done(((bf16[512,128]{1,0:T(8,128)(2,1)}), bf16[128,128]{1,0:T(8,128)(2,1)}) %reduce-scatter.2.cloned.1.call-update) | async-done | bytes 32784 | tf_op jit(solution)/shard_map/reduce_scatter | solution.py:253
  331.7 5.4 all_gather.11
  338.0 7.6 %while.138 = (s32[]{:T(128)}, f32[8,128,128]{2,1,0:T(8,128)}, s32[8,128]{1,0:T(8,128)S(1)}, f32[512,128]{1,0:T(8,128)S(1)}, s32[]{:T(128)}) while((s32[]{:T(128)}, f32[8,128,128]{2,1,0:T(8,128)}, s32[8,128]{1,0:T(8,128)S(1)}, f32[512,128]{1,0:T(8,128)S(1)}, s32[]{:T(128)}) %tuple.278), condition=%wide.region_22.23_spmd, body=%wide.region_21.22_spmd.sunk | while | flops 100728832 | bytes 329293 | solution.py:61
  346.7 2.2 fusion.111
  348.9 22.1 %while.146 = (s32[]{:T(128)}, f32[12,128,128]{2,0,1:T(8,128)}, s32[4]{0:T(128)S(1)}, s32[32]{0:T(128)S(1)}, s32[32]{0:T(128)S(1)}, /*index=5*/bf16[32,128,128]{2...) while((s32[]{:T(128)}, f32[12,128,128]{2,0,1:T(8,128)}, ...), condition=%wide.region_24.25_spmd.clone, body=%wide.region_23.24_spmd.clone.sunk | while | flops 63308196 | bytes 4981229 | solution.py:114
  351.7 1.9 convolution_add_fusion.25
  356.3 3.1 convolution_add_fusion.25
  362.1 3.1 convolution_add_fusion.25
  367.9 3.1 convolution_add_fusion.25
  373.9 4.7 collective-permute-start.6
  378.6 2.1 fusion.100
  383.8 28.3 %while.139 = (s32[]{:T(128)}, f32[16,128,128]{2,1,0:T(8,128)}, s32[16,128]{1,0:T(8,128)}, f32[1024,128]{1,0:T(8,128)S(1)}, s32[]{:T(128)}) while((s32[]{:T(128)}, f32[16,128,128]{2,1,0:T(8,128)}, s32[16,128]{1,0:T(8,128)}, f32[1024,128]{1,0:T(8,128)S(1)}, s32[]{:T(128)}) %tuple.283), condition=%wide.region_26.27_spmd, body=%wide.region_25.26_spmd.sunk | while | flops 201457664 | bytes 591437 | solution.py:61
  415.5 69.3 %while.147 = (s32[]{:T(128)}, f32[24,128,128]{2,0,1:T(8,128)S(1)}, s32[16]{0:T(128)S(1)}, s32[128]{0:T(128)S(1)}, s32[128]{0:T(128)S(1)}, /*index=5*/bf16[32,128...) while((s32[]{:T(128)}, f32[24,128,128]{2,0,1:T(8,128)S(1)}, ...), condition=%wide.region_28.29_spmd.clone, body=%wide.region_27.28_spmd.clone.sunk | while | flops 84804176 | bytes 6816321 | solution.py:114
  486.5 3.0 collective-permute-start.10
  490.9 4.5 collective-permute-start.8
  501.0 89.5 %all-reduce.6.cloned.1.call-done = f32[3,128,128]{1,2,0:T(8,128)} async-done(((f32[3,128,128]{1,2,0:T(8,128)}), f32[3,128,128]{1,2,0:T(8,128)}) %all-reduce.6.cloned.1.call-update) | async-done | bytes 196624 | tf_op jit(solution)/shard_map/psum | solution.py:337
  (736 shorter events, 319.2 us)
Async XLA Ops:
  7.2 15.8 %copy-start.14 = (bf16[2048,128]{1,0:T(8,128)(2,1)S(1)}, bf16[2048,128]{1,0:T(8,128)(2,1)}, u32[]{:S(2)}) copy-start(bf16[2048,128]{1,0:T(8,128)(2,1)} %param.45) | copy-start | bytes 1572868
  7.2 186.9 %all-reduce.8.cloned.1.call-start = ((), (), s32[]{:S(2)}) async-start(), calls=%async_computation.3 | async-start | bytes 1048576 | tf_op jit(solution)/shard_map/psum | solution.py:180
  10.5 52.4 %collective-permute-start.3 = (bf16[256,128]{1,0:T(8,128)(2,1)}, bf16[256,128]{1,0:T(8,128)(2,1)S(1)}, u32[]{:S(2)}, u32[]{:S(2)}) collective-permute-start(bf16[256,128]{1,0:T(8,128)(2,1)} %bitcast.12), channel_id=1, source_target_pairs={{1,0},{2,1},{3,2},{5,4},{6,5},{7,6},{9,8},{10,9},{11,10},{13,12},{... | collective-permute-start | bytes 196616 | tf_op jit(solution)/shard_map/ppermute | solution.py:21
  11.8 51.1 %collective-permute-start.2 = (bf16[256,128]{1,0:T(8,128)(2,1)S(1)}, bf16[256,128]{1,0:T(8,128)(2,1)S(1)}, u32[]{:S(2)}, u32[]{:S(2)}) collective-permute-start(bf16[256,128]{1,0:T(8,128)(2,1)S(1)} %bitcast.309), channel_id=1, source_target_pairs={{0,1},{1,2},{2,3},{4,5},{5,6},{6,7},{8,9},{9,10},{10,11},{12,13},{... | collective-permute-start | bytes 196616 | tf_op jit(solution)/shard_map/ppermute | solution.py:19
  14.9 48.1 %collective-permute-start.1 = (bf16[256,128]{1,0:T(8,128)(2,1)S(1)}, bf16[256,128]{1,0:T(8,128)(2,1)}, u32[]{:S(2)}, u32[]{:S(2)}) collective-permute-start(bf16[256,128]{1,0:T(8,128)(2,1)S(1)} %bitcast.308), channel_id=1, source_target_pairs={{4,0},{8,4},{12,8},{5,1},{9,5},{13,9},{6,2},{10,6},{14,10},{7,3},{... | collective-permute-start | bytes 196616 | tf_op jit(solution)/shard_map/ppermute | solution.py:21
  16.2 46.8 %collective-permute-start = (bf16[256,128]{1,0:T(8,128)(2,1)S(1)}, bf16[256,128]{1,0:T(8,128)(2,1)}, u32[]{:S(2)}, u32[]{:S(2)}) collective-permute-start(bf16[256,128]{1,0:T(8,128)(2,1)S(1)} %bitcast.307), channel_id=1, source_target_pairs={{0,4},{4,8},{8,12},{1,5},{5,9},{9,13},{2,6},{6,10},{10,14},{3,7},{... | collective-permute-start | bytes 196616 | tf_op jit(solution)/shard_map/ppermute | solution.py:19
  135.5 24.6 %copy-start.25 = (s32[4]{0:T(128)S(1)}, s32[4]{0:T(128)}, u32[]{:S(2)}) copy-start(s32[4]{0:T(128)} %param.59) | copy-start | bytes 52
  135.5 58.5 %copy-start.23 = (bf16[128,128]{1,0:T(8,128)(2,1)S(1)}, bf16[128,128]{1,0:T(8,128)(2,1)}, u32[]{:S(2)}) copy-start(bf16[128,128]{1,0:T(8,128)(2,1)} %param.47) | copy-start | bytes 98308
  159.2 42.5 %copy-start.6 = (f32[16,128,128]{2,1,0:T(8,128)}, f32[16,128,128]{2,1,0:T(8,128)S(1)}, u32[]{:S(2)}) copy-start(f32[16,128,128]{2,1,0:T(8,128)S(1)} %get-tuple-element.1454) | copy-start | bytes 3145732
  159.2 42.5 %copy-start.24 = (s32[1024]{0:T(1024)S(1)}, s32[1024]{0:T(1024)}, u32[]{:S(2)}) copy-start(s32[1024]{0:T(1024)} %param.60) | copy-start | bytes 12292
  159.2 42.5 %copy-start.28 = (s32[16]{0:T(128)S(1)}, s32[16]{0:T(128)}, u32[]{:S(2)}) copy-start(s32[16]{0:T(128)} %param.62) | copy-start | bytes 196
  159.2 44.4 %copy-start.30 = (s32[32]{0:T(128)S(1)}, s32[32]{0:T(128)}, u32[]{:S(2)}) copy-start(s32[32]{0:T(128)} %param.57) | copy-start | bytes 388
  159.2 44.4 %copy-start.31 = (s32[32]{0:T(128)S(1)}, s32[32]{0:T(128)}, u32[]{:S(2)}) copy-start(s32[32]{0:T(128)} %param.58) | copy-start | bytes 388
  159.2 44.4 %copy-start.33 = (s32[32]{0:T(128)S(1)}, s32[32]{0:T(128)}, u32[]{:S(2)}) copy-start(s32[32]{0:T(128)} %param.56) | copy-start | bytes 388
  160.0 102.0 %all-reduce.10.cloned.1.call-start = ((), (), s32[]{:S(2)}) async-start(), calls=%async_computation.4 | async-start | bytes 131072 | tf_op jit(solution)/shard_map/psum | solution.py:215
  195.8 6.2 %collective-permute-start.5 = (bf16[256,128]{1,0:T(8,128)(2,1)S(1)}, bf16[256,128]{1,0:T(8,128)(2,1)S(1)}, u32[]{:S(2)}, u32[]{:S(2)}) collective-permute-start(bf16[256,128]{1,0:T(8,128)(2,1)S(1)} %bitcast.304), channel_id=1, source_target_pairs={{4,0},{8,4},{12,8},{5,1},{9,5},{13,9},{6,2},{10,6},{14,10},{7,3},{... | collective-permute-start | bytes 196616 | tf_op jit(solution)/shard_map/ppermute | solution.py:21
  197.1 6.4 %collective-permute-start.4 = (bf16[256,128]{1,0:T(8,128)(2,1)S(1)}, bf16[256,128]{1,0:T(8,128)(2,1)S(1)}, u32[]{:S(2)}, u32[]{:S(2)}) collective-permute-start(bf16[256,128]{1,0:T(8,128)(2,1)S(1)} %bitcast.303), channel_id=1, source_target_pairs={{0,4},{4,8},{8,12},{1,5},{5,9},{9,13},{2,6},{6,10},{10,14},{3,7},{... | collective-permute-start | bytes 196616 | tf_op jit(solution)/shard_map/ppermute | solution.py:19
  203.7 14.8 %copy-start.19 = (bf16[1024,128]{1,0:T(8,128)(2,1)S(1)}, bf16[1024,128]{1,0:T(8,128)(2,1)}, u32[]{:S(2)}) copy-start(bf16[1024,128]{1,0:T(8,128)(2,1)} %get-tuple-element.717) | copy-start | bytes 786436
  203.7 14.8 %copy-start.20 = (bf16[1024,128]{1,0:T(8,128)(2,1)S(1)}, bf16[1024,128]{1,0:T(8,128)(2,1)}, u32[]{:S(2)}) copy-start(bf16[1024,128]{1,0:T(8,128)(2,1)} %get-tuple-element.718) | copy-start | bytes 786436
  222.5 39.5 %copy-start.21 = (bf16[128,128]{1,0:T(8,128)(2,1)S(1)}, bf16[128,128]{1,0:T(8,128)(2,1)}, u32[]{:S(2)}) copy-start(bf16[128,128]{1,0:T(8,128)(2,1)} %param.48) | copy-start | bytes 98308
  226.7 104.1 %reduce-scatter.2.cloned.1.call-start = ((), (), s32[]{:S(2)}) async-start(), calls=%async_computation.1 | async-start | bytes 163840 | tf_op jit(solution)/shard_map/reduce_scatter | solution.py:253
  227.6 43.3 %copy-start.17 = (bf16[4,128,128]{1,2,0:T(8,128)(2,1)}, bf16[4,128,128]{1,2,0:T(8,128)(2,1)S(1)}, u32[]{:S(2)}) copy-start(bf16[4,128,128]{1,2,0:T(8,128)(2,1)S(1)} %copy.67) | copy-start | bytes 393220
  281.6 28.3 %copy-start.18 = (bf16[4,128,128]{1,2,0:T(8,128)(2,1)S(1)}, bf16[4,128,128]{1,2,0:T(8,128)(2,1)}, u32[]{:S(2)}) copy-start(bf16[4,128,128]{1,2,0:T(8,128)(2,1)} %copy-done.17) | copy-start | bytes 393220
  310.0 20.9 %copy-start.22 = (bf16[128,128]{1,0:T(8,128)(2,1)S(1)}, bf16[128,128]{1,0:T(8,128)(2,1)}, u32[]{:S(2)}) copy-start(bf16[128,128]{1,0:T(8,128)(2,1)} %get-tuple-element.720) | copy-start | bytes 98308
  311.4 279.2 %all-reduce.6.cloned.1.call-start = ((), (), s32[]{:S(2)}) async-start(), calls=%async_computation.2 | async-start | bytes 393216 | tf_op jit(solution)/shard_map/psum | solution.py:337
  372.6 9.1 %collective-permute-start.7 = (bf16[256,128]{1,0:T(8,128)(2,1)S(1)}, bf16[256,128]{1,0:T(8,128)(2,1)S(1)}, u32[]{:S(2)}, u32[]{:S(2)}) collective-permute-start(bf16[256,128]{1,0:T(8,128)(2,1)S(1)} %bitcast.306), channel_id=1, source_target_pairs={{4,0},{8,4},{12,8},{5,1},{9,5},{13,9},{6,2},{10,6},{14,10},{7,3},{... | collective-permute-start | bytes 196616 | tf_op jit(solution)/shard_map/ppermute | solution.py:21
  373.9 7.8 %collective-permute-start.6 = (bf16[256,128]{1,0:T(8,128)(2,1)S(1)}, bf16[256,128]{1,0:T(8,128)(2,1)S(1)}, u32[]{:S(2)}, u32[]{:S(2)}) collective-permute-start(bf16[256,128]{1,0:T(8,128)(2,1)S(1)} %bitcast.305), channel_id=1, source_target_pairs={{0,4},{4,8},{8,12},{1,5},{5,9},{9,13},{2,6},{6,10},{10,14},{3,7},{... | collective-permute-start | bytes 196616 | tf_op jit(solution)/shard_map/ppermute | solution.py:19
  485.2 11.3 %collective-permute-start.11 = (bf16[256,128]{1,0:T(8,128)(2,1)S(1)}, bf16[256,128]{1,0:T(8,128)(2,1)S(1)}, u32[]{:S(2)}, u32[]{:S(2)}) collective-permute-start(bf16[256,128]{1,0:T(8,128)(2,1)S(1)} %bitcast.313), channel_id=1, source_target_pairs={{1,0},{2,1},{3,2},{5,4},{6,5},{7,6},{9,8},{10,9},{11,10},{13,12},{... | collective-permute-start | bytes 196616 | tf_op jit(solution)/shard_map/ppermute | solution.py:21
  486.5 10.0 %collective-permute-start.10 = (bf16[256,128]{1,0:T(8,128)(2,1)S(1)}, bf16[256,128]{1,0:T(8,128)(2,1)S(1)}, u32[]{:S(2)}, u32[]{:S(2)}) collective-permute-start(bf16[256,128]{1,0:T(8,128)(2,1)S(1)} %bitcast.312), channel_id=1, source_target_pairs={{0,1},{1,2},{2,3},{4,5},{5,6},{6,7},{8,9},{9,10},{10,11},{12,13},{... | collective-permute-start | bytes 196616 | tf_op jit(solution)/shard_map/ppermute | solution.py:19
  489.6 7.0 %collective-permute-start.9 = (bf16[256,128]{1,0:T(8,128)(2,1)S(1)}, bf16[256,128]{1,0:T(8,128)(2,1)S(1)}, u32[]{:S(2)}, u32[]{:S(2)}) collective-permute-start(bf16[256,128]{1,0:T(8,128)(2,1)S(1)} %bitcast.311), channel_id=1, source_target_pairs={{4,0},{8,4},{12,8},{5,1},{9,5},{13,9},{6,2},{10,6},{14,10},{7,3},{... | collective-permute-start | bytes 196616 | tf_op jit(solution)/shard_map/ppermute | solution.py:21
  490.9 6.8 %collective-permute-start.8 = (bf16[256,128]{1,0:T(8,128)(2,1)S(1)}, bf16[256,128]{1,0:T(8,128)(2,1)S(1)}, u32[]{:S(2)}, u32[]{:S(2)}) collective-permute-start(bf16[256,128]{1,0:T(8,128)(2,1)S(1)} %bitcast.310), channel_id=1, source_target_pairs={{0,4},{4,8},{8,12},{1,5},{5,9},{9,13},{2,6},{6,10},{10,14},{3,7},{... | collective-permute-start | bytes 196616 | tf_op jit(solution)/shard_map/ppermute | solution.py:19
  499.2 91.4 %copy-start.27 = (f32[3]{0:T(128)S(1)}, f32[3]{0:T(128)}, u32[]{:S(2)}) copy-start(f32[3]{0:T(128)} %constant.194.clone) | copy-start | bytes 40
  (27 other events, 82.5 us)
Sparse Core Ops, SparseCore 0:
  160.1 33.8 all-reduce.7
  226.8 35.1 all-reduce.9
  311.5 19.2 reduce-scatter.1
  500.0 90.4 all-reduce.5
where the time goes:
time: 603 us; the launch traced here: 599 us
  matrix products  212 us (35%)
  waiting for transfers between devices  178 us (30%)
  local copies, waits for them, and re-layouts  89.5 us (15%)
  starting transfers between devices  33.9 us (6%)
  loops' own time  29.2 us (5%)
  other arithmetic  24.8 us (4%)
  blocking collectives  16.4 us (3%)
  between operations  15.4 us (3%)
    psum x1, waiting for transfers between devices, local(): lax.psum(jnp.stack([fine_grad, middle_grad, top_grad]), ('row', 'col'))  89.5 us
    dot_general x44, matrix products, add_blocks(): jnp.einsum('tb,tih->bih', selector, products, precision=lax.Precision.HIG...  57.9 us
    dot_general x82, matrix products, select_blocks(): jnp.einsum('ts,sjh->tjh', selector, stack, preferred_element_type=jnp.flo...  47.1 us
    eq x96, local copies, waits for them, and re-layouts, one_hot_rows(): index[:, None] == jnp.arange(extent, dtype=jnp.int32)[None, :]  44.6 us
    dot_general x48, matrix products, take_block(): return jnp.dot(selector, table, precision=lax.Precision.HIGHEST)  44.4 us
    dot_general x48, matrix products, add_block(): jnp.dot(table.T, block_values, precision=lax.Precision.HIGHEST)  44.1 us
    psum x1, waiting for transfers between devices, local(): lax.psum(partial_top.astype(jnp.bfloat16), 'row').astype(jnp.float32)  34.3 us
    psum x1, waiting for transfers between devices, local(): lax.psum(pooled.astype(jnp.bfloat16), 'col').astype(jnp.float32)  34 us
  transfers between devices with their start and end apart: 16, of which 7 were waited for; matrix products, arithmetic and copies ran while one was open for 8% of the time, Pallas kernels for 0%

commit v1 on v0

v1 whole, which is shorter than its diff:
```python
import functools

import jax
import jax.numpy as jnp
from jax import lax
from jax.experimental import pallas as pl
from jax.experimental.pallas import tpu as pltpu
from jax.sharding import PartitionSpec as P

MESH = pl.DeviceIdType.MESH
F32 = jnp.float32
BF16 = jnp.bfloat16
UNROLL = 8


def gelu_pair(x):
    k = 0.7978845608028654
    a = 0.044715
    square = x * x
    t = jnp.tanh(k * (x + a * (square * x)))
    half = 0.5 + 0.5 * t
    slope = half + (0.5 * k) * x * ((1.0 - t * t) * (1.0 + (3.0 * a) * square))
    return x * half, slope


def mm(a, b):
    return jnp.dot(a, b, preferred_element_type=F32)


def mm_tn(a, b):
    return lax.dot_general(a, b, (((0,), (0,)), ((), ())), preferred_element_type=F32)


def mm_nt(a, b):
    return lax.dot_general(a, b, (((1,), (1,)), ((), ())), preferred_element_type=F32)


def loop(count, body, unroll=1):
    while count % unroll:
        unroll //= 2

    def step(index, carry):
        for inner in range(unroll):
            body(index * unroll + inner)
        return carry

    lax.fori_loop(0, count // unroll, step, 0)


def kernel(
    dims,
    prev,
    last,
    fine_source,
    fine_target,
    fine_kind,
    fine_sends,
    middle_source,
    middle_target,
    middle_kind,
    middle_sends,
    top_source,
    top_kind,
    feat,
    cot,
    w_fine,
    w_middle,
    w_top,
    bank,
    fine_pool,
    middle_pool,
    fine_out,
    grad_out,
    weight_out,
    bank_t,
    pool_map,
    pick_map,
    chain,
    ext,
    send_fine,
    back_fine,
    home_fine,
    hidden,
    slope,
    grad_hidden,
    grad_sum,
    grad_blocks,
    part_h,
    part_g,
    slots_h,
    slots_g,
    full_h,
    full_g,
    m_ext,
    m_send,
    m_back,
    m_home,
    m_hidden,
    m_slope,
    m_grad,
    m_low,
    m_gsum,
    m_gmsg,
    table,
    top_slots_h,
    top_slots_g,
    top_h,
    top_g,
    t_msg,
    t_gsum,
    t_slope,
    t_gmsg,
    t_table,
    mg_slots,
    fg_slots_col,
    fg_slots_row,
    send_sem,
    recv_sem,
):
    n_row, n_col, send, m_send_n, t_slots = dims
    r = lax.axis_index("row")
    c = lax.axis_index("col")
    place = {"row": (r, n_row), "col": (c, n_col)}
    kinds, bs, width = bank.shape
    rows = feat.shape[0]
    blocks = rows // bs
    m_rows = m_low.shape[0]
    m_blocks = m_rows // bs
    t_rows = n_col * bs
    chunk = m_rows // n_col
    p2 = (m_rows / (rows * n_col)) ** 0.5
    p3 = (t_rows / (m_rows * n_row)) ** 0.5
    allotted = [0]

    def semaphores(count):
        base = allotted[0]
        allotted[0] += count
        return base

    def remote(src, dst, s, v, axis, target):
        return pltpu.make_async_remote_copy(
            src_ref=src,
            dst_ref=dst,
            send_sem=send_sem.at[s],
            recv_sem=recv_sem.at[v],
            device_id={axis: target},
            device_id_type=MESH,
        )

    class Exchange:
        def __init__(self, source, slots, axis):
            self.source, self.slots, self.axis = source, slots, axis
            self.me, self.n = place[axis]
            self.base = semaphores(self.n)

        def start(self):
            for k in range(1, self.n):
                p = lax.rem(self.me + k, self.n)
                remote(
                    self.source(p),
                    self.slots.at[self.me],
                    self.base + k,
                    self.base + self.me,
                    self.axis,
                    p,
                ).start()

        def wait(self):
            for k in range(1, self.n):
                p = lax.rem(self.me + k, self.n)
                remote(
                    self.source(p),
                    self.slots.at[p],
                    self.base + k,
                    self.base + p,
                    self.axis,
                    p,
                ).wait()

        def total(self):
            value = self.slots[0].astype(F32)
            for k in range(1, self.n):
                value = value + self.slots[k].astype(F32)
            return value

    class Shift:
        def __init__(self, source, target, axis, delta):
            self.me, self.n = place[axis]
            self.base = semaphores(1)
            self.copy = lambda p: remote(source, target, self.base, self.base, axis, p)
            self.delta = delta
            low, high = self.me > 0, self.me < self.n - 1
            self.sends, self.gets = (high, low) if delta > 0 else (low, high)
            self.lacks = jnp.logical_not(self.gets)
            self.target = target

        def clear(self):
            @pl.when(self.lacks)
            def _():
                self.target[...] = jnp.zeros(self.target.shape, BF16)

        def start(self):
            @pl.when(self.sends)
            def _():
                self.copy(self.me + self.delta).start()

        def wait(self):
            other = jnp.clip(self.me + self.delta, 0, self.n - 1)

            @pl.when(self.sends)
            def _():
                self.copy(other).wait_send()

            @pl.when(self.gets)
            def _():
                self.copy(other).wait_recv()

    ways = (("row", 1), ("row", -1), ("col", 1), ("col", -1))
    halo = [
        Shift(send_fine.at[k], ext.at[pl.ds(blocks + send * k, send)], axis, delta)
        for k, (axis, delta) in enumerate(ways)
    ]
    home = [
        Shift(back_fine.at[k], home_fine.at[k], axis, -delta)
        for k, (axis, delta) in enumerate(ways)
    ]
    m_halo = [
        Shift(
            m_send.at[k], m_ext.at[pl.ds(m_blocks + m_send_n * k, m_send_n)], axis, delta
        )
        for k, (axis, delta) in enumerate(ways[:2])
    ]
    m_homes = [
        Shift(m_back.at[k], m_home.at[k], axis, -delta)
        for k, (axis, delta) in enumerate(ways[:2])
    ]
    scatter_h = Exchange(lambda p: part_h.at[p], slots_h, "col")
    scatter_g = Exchange(lambda p: part_g.at[p], slots_g, "col")
    gather_h = Exchange(lambda p: full_h.at[c], full_h, "col")
    gather_g = Exchange(lambda p: full_g.at[c], full_g, "col")
    rows_h = Exchange(lambda p: top_slots_h.at[r], top_slots_h, "row")
    rows_g = Exchange(lambda p: top_slots_g.at[r], top_slots_g, "row")
    cols_h = Exchange(lambda p: top_h.at[c], top_h, "col")
    cols_g = Exchange(lambda p: top_g.at[c], top_g, "col")
    sum_middle = Exchange(lambda p: mg_slots.at[r], mg_slots, "row")
    sum_fine_col = Exchange(lambda p: fg_slots_col.at[c], fg_slots_col, "col")
    sum_fine_row = Exchange(lambda p: fg_slots_row.at[r], fg_slots_row, "row")

    barrier = pltpu.get_barrier_semaphore()
    for axis in ("row", "col"):
        me, n = place[axis]
        for k in range(1, n):
            pl.semaphore_signal(
                barrier, inc=1, device_id={axis: lax.rem(me + k, n)}, device_id_type=MESH
            )
    for item in halo + home + m_halo + m_homes:
        item.clear()
    chain[0] = jnp.zeros((bs, width), F32)

    def message(b):
        value = mm(feat[pl.ds(pl.multiple_of(b * bs, bs), bs), :], w_fine[...]).astype(BF16)
        ext[b] = value
        grad_blocks[b] = value

    loop(blocks, message, 4)
    for k in range(4):
        for i in range(send):
            send_fine[k, i] = grad_blocks[fine_sends[k * send + i]]
    pl.semaphore_wait(barrier, n_row + n_col - 2)
    for item in halo:
        item.start()

    def pool_block(j):
        index = fine_pool[pl.ds(j, 1), :]
        for i in range(m_blocks):
            ids = lax.broadcasted_iota(jnp.int32, (bs, bs), 0) + i * bs
            pool_map[i * bs : (i + 1) * bs, pl.ds(pl.multiple_of(j * bs, bs), bs)] = jnp.where(
                ids == index, 1.0, 0.0
            ).astype(BF16)

    loop(blocks, pool_block)

    def pool_into(part, values):
        def one(m):
            part[m] = mm(pool_map[pl.ds(pl.multiple_of(m * chunk, chunk), chunk), :], values[...]).astype(
                BF16
            )

        loop(n_col, one)

    pool_into(part_g, cot)
    slots_g[c] = part_g[c]
    scatter_g.start()

    def flip(k):
        bank_t[k] = bank[k].astype(F32).T.astype(BF16)

    loop(kinds, flip, 4)
    for item in halo:
        item.wait()
    scatter_g.wait()
    full_g[c] = scatter_g.total().astype(BF16)
    gather_g.start()

    def fine_slot(t):
        chain[t + 1] = mm(bank[fine_kind[t]], ext[fine_source[t]]) + chain[prev[0, t]]

    loop(fine_kind.shape[0], fine_slot, UNROLL)

    def fine_state(b):
        at = pl.ds(pl.multiple_of(b * bs, bs), bs)
        value, rate = gelu_pair(chain[last[0, b]])
        state = feat[at, :].astype(F32) + value
        hidden[at, :] = state
        slope[at, :] = rate
        grad_sum[at, :] = state.astype(BF16)

    loop(blocks, fine_state)
    pool_into(part_h, grad_sum)
    slots_h[c] = part_h[c]
    scatter_h.start()

    gather_g.wait()
    for k in range(n_col):
        m_gsum[k * chunk : (k + 1) * chunk, :] = full_g[k].astype(F32) * p2

    def top_partial(values):
        maps = []
        for j in range(m_blocks):
            ids = lax.broadcasted_iota(jnp.int32, (bs, bs), 0) + c * bs
            maps.append(jnp.where(ids == middle_pool[j : j + 1, :], 1.0, 0.0).astype(BF16))
        return mm(jnp.concatenate(maps, axis=1), values)

    top_slots_g[r] = top_partial(m_gsum[...].astype(BF16)).astype(BF16)
    rows_g.start()

    def pick_block(j):
        index = jnp.broadcast_to(fine_pool[pl.ds(j, 1), :].astype(F32), (bs, bs)).T
        for i in range(m_blocks):
            ids = (lax.broadcasted_iota(jnp.int32, (bs, bs), 1) + i * bs).astype(F32)
            pick_map[pl.ds(pl.multiple_of(j * bs, bs), bs), i * bs : (i + 1) * bs] = jnp.where(
                ids == index, 1.0, 0.0
            ).astype(BF16)

    scatter_h.wait()
    full_h[c] = scatter_h.total().astype(BF16)
    gather_h.start()
    loop(blocks, pick_block)
    rows_g.wait()
    top_g[c] = (rows_g.total() * p3).astype(BF16)
    cols_g.start()
    gather_h.wait()

    for k in range(n_col):
        at = slice(k * chunk, (k + 1) * chunk)
        value = full_h[k].astype(F32) * p2
        m_hidden[at, :] = value
        m_low[at, :] = value.astype(BF16)
    for b in range(m_blocks):
        value = mm(m_low[b * bs : (b + 1) * bs, :], w_middle[...]).astype(BF16)
        m_ext[b] = value
        m_grad[b] = value
    for k in range(2):
        for i in range(m_send_n):
            m_send[k, i] = m_grad[middle_sends[k * m_send_n + i]]
    for item in m_halo:
        item.start()
    cols_g.wait()
    for item in m_halo:
        item.wait()

    def middle_slot(t):
        chain[t + 1] = mm(bank[middle_kind[t]], m_ext[middle_source[t]]) + chain[prev[2, t]]

    loop(middle_kind.shape[0], middle_slot, UNROLL)

    def middle_state(b):
        at = pl.ds(pl.multiple_of(b * bs, bs), bs)
        value, rate = gelu_pair(chain[last[2, b]])
        m_hidden[at, :] = m_hidden[at, :] + value
        m_slope[at, :] = rate

    loop(m_blocks, middle_state)
    top_slots_h[r] = top_partial(m_hidden[...].astype(BF16)).astype(BF16)
    rows_h.start()
    rows_h.wait()
    top_h[c] = (rows_h.total() * p3).astype(BF16)
    cols_h.start()
    cols_h.wait()

    def top_message(b):
        t_msg[b] = mm(top_h[b], w_top[...]).astype(BF16)

    loop(n_col, top_message)

    def top_state(b):
        total = jnp.zeros((bs, width), F32)
        for s in range(t_slots):
            t = b * t_slots + s
            total = total + mm(bank[top_kind[t]], t_msg[top_source[t]])
        value, rate = gelu_pair(total)
        at = pl.ds(pl.multiple_of(b * bs, bs), bs)
        t_table[at, :width] = (top_h[b].astype(F32) + value).astype(BF16)
        t_gsum[b] = (top_g[b].astype(F32) * rate).astype(BF16)

    loop(n_col, top_state)

    def top_back(b):
        for s in range(t_slots):
            t = b * t_slots + s
            chain[t + 1] = mm(bank_t[top_kind[t]], t_gsum[b]) + chain[prev[4, t]]

    loop(n_col, top_back)

    def top_grad(b):
        at = pl.ds(pl.multiple_of(b * bs, bs), bs)
        message_grad = chain[last[4, b]].astype(BF16)
        t_gmsg[at, :] = message_grad
        t_table[at, width:] = (
            top_g[b].astype(F32) + mm_nt(message_grad, w_top[...])
        ).astype(BF16)

    loop(n_col, top_grad)

    def middle_pick(j):
        at = pl.ds(pl.multiple_of(j * bs, bs), bs)
        index = jnp.broadcast_to(middle_pool[pl.ds(j, 1), :].astype(F32), (bs, bs)).T
        maps = []
        for i in range(n_col):
            ids = (lax.broadcasted_iota(jnp.int32, (bs, bs), 1) + i * bs).astype(F32)
            maps.append(jnp.where(ids == index, 1.0, 0.0).astype(BF16))
        picked = mm(jnp.concatenate(maps, axis=1), t_table[...]) * p3
        table[at, :] = (m_hidden[at, :] + picked[:, :width]).astype(BF16)
        grad = m_gsum[at, :] + picked[:, width:]
        m_gsum[at, :] = grad
        m_grad[j] = (grad * m_slope[at, :]).astype(BF16)

    loop(m_blocks, middle_pick)

    def middle_back(t):
        chain[t + 1] = mm(bank_t[middle_kind[t]], m_grad[middle_target[t]]) + chain[prev[3, t]]

    m_count = middle_kind.shape[0]
    loop(m_count, middle_back, UNROLL)
    for k in range(2):
        for i in range(m_send_n):
            m_back[k, i] = chain[last[3, m_blocks + k * m_send_n + i]].astype(BF16)
    for item in m_homes:
        item.start()

    pair = 2
    wide = pair * bs

    def fine_pick(j):
        at = pl.ds(pl.multiple_of(j * wide, wide), wide)
        fine_out[at, :] = (hidden[at, :] + p2 * mm(pick_map[at, :], table[...])).astype(BF16)

    loop(rows // wide, fine_pick)
    weight_out[2] = mm_tn(top_h[...].reshape(t_rows, width), t_gmsg[...]) * t_rows ** (-0.5)
    for item in m_homes:
        item.wait()
    for k in range(2):
        for i in range(m_send_n):
            t = m_count + k * m_send_n + i
            chain[t + 1] = m_home[k, i].astype(F32) + chain[prev[3, t]]

    def middle_grad(b):
        at = pl.ds(pl.multiple_of(b * bs, bs), bs)
        message_grad = chain[last[3, b]].astype(BF16)
        m_gmsg[at, :] = message_grad
        table[at, :] = (m_gsum[at, :] + mm_nt(message_grad, w_middle[...])).astype(BF16)

    loop(m_blocks, middle_grad)
    mg_slots[r] = (mm_tn(m_low[...], m_gmsg[...]) * (m_rows * n_row) ** (-0.5)).astype(BF16)
    sum_middle.start()

    def fine_grad_pick(j):
        at = pl.ds(pl.multiple_of(j * wide, wide), wide)
        grad = cot[at, :].astype(F32) + p2 * mm(pick_map[at, :], table[...])
        grad_hidden[at, :] = grad
        grad = (grad * slope[at, :]).astype(BF16)
        grad_blocks[pl.ds(j * pair, pair)] = grad.reshape(pair, bs, width)

    loop(rows // wide, fine_grad_pick)

    f_count = fine_kind.shape[0]

    def fine_back(t):
        chain[t + 1] = mm(bank_t[fine_kind[t]], grad_blocks[fine_target[t]]) + chain[prev[1, t]]

    loop(f_count, fine_back, UNROLL)
    for k in range(4):
        for i in range(send):
            back_fine[k, i] = chain[last[1, blocks + k * send + i]].astype(BF16)
    for item in home:
        item.start()
    sum_middle.wait()
    weight_out[1] = sum_middle.total()
    for item in home:
        item.wait()
    for k in range(4):
        for i in range(send):
            t = f_count + k * send + i
            chain[t + 1] = home_fine[k, i].astype(F32) + chain[prev[1, t]]

    def fine_message_grad(b):
        at = pl.ds(pl.multiple_of(b * bs, bs), bs)
        grad_sum[at, :] = chain[last[1, b]].astype(BF16)

    loop(blocks, fine_message_grad)
    scale = (rows * n_row * n_col) ** (-0.5)
    fg_slots_col[c] = (mm_tn(feat[...], grad_sum[...]) * scale).astype(BF16)
    sum_fine_col.start()

    def fine_final(b):
        at = pl.ds(pl.multiple_of(b * bs, bs), bs)
        grad_out[at, :] = (grad_hidden[at, :] + mm_nt(grad_sum[at, :], w_fine[...])).astype(BF16)

    loop(blocks // 2, fine_final)
    sum_fine_col.wait()
    fg_slots_row[r] = sum_fine_col.total().astype(BF16)
    sum_fine_row.start()
    loop(blocks // 2, lambda b: fine_final(b + blocks // 2))
    sum_fine_row.wait()
    weight_out[0] = sum_fine_row.total()


def links(keys, live, extent):
    pos = jnp.arange(keys.shape[1], dtype=jnp.int32)
    valid = live[:, None, :]
    same = (keys[:, :, None] == keys[:, None, :]) & (pos[None, None, :] < pos[None, :, None]) & valid
    prev = jnp.max(jnp.where(same, pos + 1, 0), axis=2)
    ids = jnp.arange(extent, dtype=jnp.int32)
    ends = (keys[:, None, :] == ids[None, :, None]) & valid
    last = jnp.max(jnp.where(ends, pos + 1, 0), axis=2)
    return prev, last


def local(
    features,
    cotangent,
    fine_weight,
    middle_weight,
    top_weight,
    tile_bank,
    fine_source,
    fine_target,
    fine_kind,
    tile_count,
    fine_sends,
    fine_pool,
    middle_source,
    middle_target,
    middle_kind,
    middle_sends,
    middle_pool,
    top_source,
    top_kind,
):
    n_row = lax.axis_size("row")
    n_col = lax.axis_size("col")
    bs = tile_bank.shape[1]
    kinds = tile_bank.shape[0]
    rows, width = features.shape
    blocks = rows // bs
    send = fine_sends.shape[0] // 4
    m_rows = middle_pool.shape[0]
    m_blocks = m_rows // bs
    m_send = middle_sends.shape[0] // 2
    t_slots = top_source.shape[0] // n_col
    chunk = m_rows // n_col
    f_count = fine_kind.shape[0]
    length = f_count + 4 * send
    extent = max(blocks + 4 * send, m_blocks + 2 * m_send, n_col)

    def padded(*pieces):
        key = jnp.concatenate(pieces)
        return jnp.pad(key, (0, length - key.shape[0]), constant_values=-1)

    keys = jnp.stack(
        [
            padded(fine_target),
            padded(fine_source, fine_sends),
            padded(middle_target),
            padded(middle_source, middle_sends),
            padded(top_source),
        ]
    )
    pos = jnp.arange(length, dtype=jnp.int32)
    alive = (pos < tile_count[0]) | (pos >= f_count)
    level = jnp.arange(5, dtype=jnp.int32)
    live = alive[None, :] | (level[:, None] >= 2)
    prev, last = links(keys, live, extent)

    def block_buf(*lead):
        return pltpu.VMEM(lead + (bs, width), BF16)

    def wide_buf(count, dtype):
        return pltpu.VMEM((count, width), dtype)

    part = pltpu.VMEM((n_col, chunk, width), BF16)
    n_sem = 12 + 8 * n_col + 4 * n_row
    scratch = [
        block_buf(kinds),
        pltpu.VMEM((m_rows, rows), BF16),
        pltpu.VMEM((rows, m_rows), BF16),
        pltpu.VMEM((length + 1, bs, width), F32),
        block_buf(blocks + 4 * send),
        block_buf(4, send),
        block_buf(4, send),
        block_buf(4, send),
        wide_buf(rows, F32),
        wide_buf(rows, F32),
        wide_buf(rows, F32),
        wide_buf(rows, BF16),
        block_buf(blocks),
        part,
        part,
        part,
        part,
        part,
        part,
        block_buf(m_blocks + 2 * m_send),
        block_buf(2, m_send),
        block_buf(2, m_send),
        block_buf(2, m_send),
        wide_buf(m_rows, F32),
        wide_buf(m_rows, F32),
        block_buf(m_blocks),
        wide_buf(m_rows, BF16),
        wide_buf(m_rows, F32),
        wide_buf(m_rows, BF16),
        wide_buf(m_rows, BF16),
        block_buf(n_row),
        block_buf(n_row),
        block_buf(n_col),
        block_buf(n_col),
        block_buf(n_col),
        block_buf(n_col),
        pltpu.VMEM((8, width), F32),
        wide_buf(n_col * bs, BF16),
        pltpu.VMEM((n_col * bs, 2 * width), BF16),
        block_buf(n_row),
        block_buf(n_col),
        block_buf(n_row),
        pltpu.SemaphoreType.DMA((n_sem,)),
        pltpu.SemaphoreType.DMA((n_sem,)),
    ]
    smem = pl.BlockSpec(memory_space=pltpu.SMEM)
    vmem = pl.BlockSpec(memory_space=pltpu.VMEM)
    return pl.pallas_call(
        functools.partial(kernel, (n_row, n_col, send, m_send, t_slots)),
        out_shape=(
            jax.ShapeDtypeStruct((rows, width), BF16),
            jax.ShapeDtypeStruct((rows, width), BF16),
            jax.ShapeDtypeStruct((3, width, width), F32),
        ),
        in_specs=[smem] * 12 + [vmem] * 8,
        out_specs=(vmem, vmem, vmem),
        scratch_shapes=scratch,
        compiler_params=pltpu.CompilerParams(
            collective_id=0, has_side_effects=True, vmem_limit_bytes=48 * 1024 * 1024
        ),
        cost_estimate=pl.CostEstimate(
            flops=4_000_000_000, bytes_accessed=4_000_000, transcendentals=400_000
        ),
    )(
        prev,
        last,
        fine_source,
        fine_target,
        fine_kind,
        fine_sends,
        middle_source,
        middle_target,
        middle_kind,
        middle_sends,
        top_source,
        top_kind,
        features,
        cotangent,
        fine_weight,
        middle_weight,
        top_weight,
        tile_bank,
        fine_pool.reshape(blocks, bs),
        middle_pool.reshape(m_blocks, bs),
    )


def solution(mesh):
    everywhere = P(("group", "row", "col"))
    by_row = P(("group", "row"))
    in_specs = (
        (P(("group", "row", "col"), None),) * 2
        + (P(),) * 4
        + (everywhere,) * 6
        + (by_row,) * 5
        + (P("group"),) * 2
    )
    out_specs = (
        P(("group", "row", "col"), None),
        P(("group", "row", "col"), None),
        P("group", None, None),
    )
    return jax.shard_map(local, mesh=mesh, in_specs=in_specs, out_specs=out_specs, check_vma=False)
```

time: 603 us -> 82.1 us (0.14)
  matrix products: 212 us -> 0 us
  waiting for transfers between devices: 178 us -> 0 us
  local copies, waits for them, and re-layouts: 89.5 us -> 9.21 us
  Pallas kernels: 0 us -> 70.3 us
  starting transfers between devices: 33.9 us -> 0 us
  loops' own time: 29.2 us -> 0 us
  other arithmetic: 24.8 us -> 0.78 us
  blocking collectives: 16.4 us -> 0 us
  between operations: 15.4 us -> 1.43 us
    dot_general x273 -> x0, matrix products: 212 us -> none  [the longest x44 57.9 us: add_blocks(): jnp.einsum('tb,tih->bih', selector, products, precision=lax.Precision.HIG...]
    psum x3 -> x0, waiting for transfers between devices: 158 us -> none  [the longest x1 89.5 us: local(): lax.psum(jnp.stack([fine_grad, middle_grad, top_grad]), ('row', 'col'))]
    pallas_call x0 -> x1, Pallas kernels: none -> 70.3 us  [local(): pl.pallas_call(functools.partial(kernel, (n_row, n_col, send, m_send, t_s...]
    eq x96 -> x0, local copies, waits for them, and re-layouts: 44.6 us -> none  [one_hot_rows(): index[:, None] == jnp.arange(extent, dtype=jnp.int32)[None, :]]
    ppermute x12 -> x0, starting transfers between devices: 33.8 us -> none  [the longest x6 26 us: extended_2(): lax.ppermute(tail, axis, [(i, (i + 1) % count) for i in range(ends)])]
    dynamic_slice x162 -> x0, local copies, waits for them, and re-layouts: 32.9 us -> none  [the longest x40 23.5 us: tile_forward(): lax.scan(add_group, initial, jnp.arange(count // group, dtype=jnp.int32))]
    another operation x12 -> x0, loops' own time: 29.2 us -> none  [the longest x2 13.9 us: tile_forward(): lax.scan(add_group, initial, jnp.arange(count // group, dtype=jnp.int32))]
    reduce_scatter x1 -> x0, waiting for transfers between devices: 17.1 us -> none  [local(): lax.psum_scatter(back_terms.astype(jnp.bfloat16), 'col', scatter_dimensio...]
  transfers between devices with their start and end apart: 16 -> 0, of which waited for: 7 -> 0; matrix products, arithmetic and copies ran while one was open for 8% -> 0% of each run, Pallas kernels for 0% -> 0%
where the time goes in v1:
time: 82.1 us; the launch traced here: 81.7 us
  Pallas kernels  70.3 us (86%)
  local copies, waits for them, and re-layouts  9.21 us (11%)
  between operations  1.43 us (2%)
    pallas_call x1, Pallas kernels, local(): pl.pallas_call(functools.partial(kernel, (n_row, n_col, send, m_send, t_s...  70.3 us
    unnamed x39, local copies, waits for them, and re-layouts  9.17 us

profile of v1, /device:TPU:0, one launch (start us, length us, event | category | flops | bytes accessed | tf_op | source)
XLA Modules:
  0.0 81.7 jit_solution(2551058551982740305)
XLA Ops:
  1.3 0.0 copy-start.13
  1.3 0.0 copy-start.14
  1.3 0.6 copy-done.13
  1.9 0.0 copy-done.14
  2.0 0.1 pad_add_fusion.1
  2.1 0.1 broadcast_or_fusion
  2.1 0.6 copy-done.1
  2.8 0.0 copy-done.2
  2.8 0.7 copy-done
  3.5 0.7 copy-done.3
  4.1 0.7 copy-done.4
  4.8 0.2 select_reduce_fusion.1.last
  5.0 0.0 copy-start.9
  5.0 0.0 copy-start.8
  5.1 0.0 copy-start.11
  5.1 0.0 copy-start.12
  5.1 0.0 copy-start.15
  5.1 0.0 copy-start.16
  5.1 0.0 copy-start.17
  5.1 0.4 select_reduce_fusion.prev
  5.5 0.0 copy-done.10
  5.6 0.2 copy-done.9
  5.8 0.0 copy-done.8
  5.8 0.0 copy-done.12
  5.8 0.0 copy-start.5
  5.8 1.2 %copy-done.5 = bf16[32,128,128]{2,1,0:T(8,128)(2,1)S(1)} copy-done((bf16[32,128,128]{2,1,0:T(8,128)(2,1)S(1)}, bf16[32,128,128]{2,1,0:T(8,128)(2,1)}, u32[]{:S(2)}) %copy-start.5) | copy-done | bytes 1048600
  7.1 1.0 %copy-done.6 = bf16[2048,128]{1,0:T(8,128)(2,1)S(1)} copy-done((bf16[2048,128]{1,0:T(8,128)(2,1)S(1)}, bf16[2048,128]{1,0:T(8,128)(2,1)}, u32[]{:S(2)}) %copy-start.6) | copy-done | bytes 524312
  8.1 1.0 %copy-done.7 = bf16[2048,128]{1,0:T(8,128)(2,1)S(1)} copy-done((bf16[2048,128]{1,0:T(8,128)(2,1)S(1)}, bf16[2048,128]{1,0:T(8,128)(2,1)}, u32[]{:S(2)}) %copy-start.7) | copy-done | bytes 524312
  9.1 70.3 %shard_map.202 = (bf16[2048,128]{1,0:T(8,128)(2,1)S(1)}, bf16[2048,128]{1,0:T(8,128)(2,1)S(1)}, f32[3,128,128]{2,1,0:T(8,128)S(1)}) custom-call(s32[5,136]{1,0:T(8,128)S(1)} %select_reduce_fusion.prev, s32[5,24]{1,0:T(8,128)S(1)} %select_reduce_fusion.1.last, s32[128]{0:T(128)S(1)} %copy-done.2, s32[128]{0:T(128)S(1)} %copy-done, s32[128]{0:T(128)S(1)} %copy-done.15, ...), custom_call_target="tpu_custom_call" | custom-call | flops 4000000000 | bytes 4000000 | tf_op jit(solution)/shard_map/pallas_call | solution.py:651
  79.4 0.8 copy.26
  80.2 0.8 copy.27
  81.0 0.7 copy.28
  (22 shorter events, 0.1 us)
Async XLA Ops:
  1.3 0.7 copy-start.13
  1.3 0.7 copy-start.14
  2.1 0.7 copy-start.1
  2.1 0.7 copy-start.2
  2.8 0.7 copy-start
  3.5 0.7 copy-start.3
  4.1 0.7 copy-start.4
  4.8 0.8 copy-start.10
  5.0 0.8 copy-start.9
  5.0 0.8 copy-start.8
  5.1 0.8 copy-start.11
  5.1 0.7 copy-start.12
  5.1 0.7 copy-start.15
  5.1 0.7 copy-start.16
  5.1 0.7 copy-start.17
  5.8 1.2 %copy-start.5 = (bf16[32,128,128]{2,1,0:T(8,128)(2,1)S(1)}, bf16[32,128,128]{2,1,0:T(8,128)(2,1)}, u32[]{:S(2)}) copy-start(bf16[32,128,128]{2,1,0:T(8,128)(2,1)} %bank.1) | copy-start | bytes 3145732
  7.1 1.0 %copy-start.6 = (bf16[2048,128]{1,0:T(8,128)(2,1)S(1)}, bf16[2048,128]{1,0:T(8,128)(2,1)}, u32[]{:S(2)}) copy-start(bf16[2048,128]{1,0:T(8,128)(2,1)} %feat.1) | copy-start | bytes 1572868
  8.1 1.0 %copy-start.7 = (bf16[2048,128]{1,0:T(8,128)(2,1)S(1)}, bf16[2048,128]{1,0:T(8,128)(2,1)}, u32[]{:S(2)}) copy-start(bf16[2048,128]{1,0:T(8,128)(2,1)} %cot.1) | copy-start | bytes 1572868

commit v2 on v1

--- a/solution.py
+++ b/solution.py
@@ -49,8 +49,7 @@
 
 def kernel(
     dims,
-    prev,
-    last,
+    tile_count,
     fine_source,
     fine_target,
     fine_kind,
@@ -61,6 +60,30 @@
     middle_sends,
     top_source,
     top_kind,
+    *refs,
+):
+    n = 15
+    inputs, results, held = refs[:n], refs[n : n + 3], refs[n + 3 : 2 * n + 3]
+    run(dims, tile_count, fine_source, fine_target, fine_kind, fine_sends, middle_source,
+        middle_target, middle_kind, middle_sends, top_source, top_kind, inputs, held,
+        *held[:8], *results, *refs[2 * n + 3 :])
+
+
+def run(
+    dims,
+    tile_count,
+    fine_source,
+    fine_target,
+    fine_kind,
+    fine_sends,
+    middle_source,
+    middle_target,
+    middle_kind,
+    middle_sends,
+    top_source,
+    top_kind,
+    inputs,
+    held,
     feat,
     cot,
     w_fine,
@@ -108,12 +131,17 @@
     top_g,
     t_msg,
     t_gsum,
-    t_slope,
     t_gmsg,
     t_table,
     mg_slots,
     fg_slots_col,
     fg_slots_row,
+    top_map,
+    middle_map,
+    key_rows,
+    link_rows,
+    link,
+    load_sem,
     send_sem,
     recv_sem,
 ):
@@ -153,9 +181,19 @@
             self.me, self.n = place[axis]
             self.base = semaphores(self.n)
 
-        def start(self):
-            for k in range(1, self.n):
-                p = lax.rem(self.me + k, self.n)
+        def peers(self):
+            me, n = self.me, self.n
+            if self.axis == "row" or n % 2:
+                return [lax.rem(me + k, n) for k in range(1, n)]
+            chip, core = me // 2, me % 2
+            away = [
+                lax.rem(chip + d, n // 2) * 2 + e for d in range(1, n // 2) for e in range(2)
+            ]
+            return away + [chip * 2 + 1 - core]
+
+        def start(self, before=lambda p: None):
+            for k, p in enumerate(self.peers()):
+                before(p)
                 remote(
                     self.source(p),
                     self.slots.at[self.me],
@@ -166,8 +204,7 @@
                 ).start()
 
         def wait(self):
-            for k in range(1, self.n):
-                p = lax.rem(self.me + k, self.n)
+            for k, p in enumerate(self.peers()):
                 remote(
                     self.source(p),
                     self.slots.at[p],
@@ -253,6 +290,13 @@
             pl.semaphore_signal(
                 barrier, inc=1, device_id={axis: lax.rem(me + k, n)}, device_id_type=MESH
             )
+    loads = [
+        pltpu.make_async_copy(src, dst, load_sem.at[k])
+        for k, (src, dst) in enumerate(zip(inputs, held))
+    ]
+    order = [0, 2, 6, 1, 5, 7, 8, 9, 10, 11, 12, 13, 14, 3, 4]
+    for k in order:
+        loads[k].start()
     for item in halo + home + m_halo + m_homes:
         item.clear()
     chain[0] = jnp.zeros((bs, width), F32)
@@ -262,6 +306,8 @@
         ext[b] = value
         grad_blocks[b] = value
 
+    loads[0].wait()
+    loads[2].wait()
     loop(blocks, message, 4)
     for k in range(4):
         for i in range(send):
@@ -270,6 +316,50 @@
     for item in halo:
         item.start()
 
+    for k in order[2:]:
+        loads[k].wait()
+
+    keys_f, keys_b, keys_bs, keys_m, keys_n, keys_ns, keys_t = held[8:]
+    first = lax.broadcasted_iota(jnp.int32, (bs, bs), 0)
+    second = lax.broadcasted_iota(jnp.int32, (bs, bs), 1)
+
+    def spread(ref, line):
+        key_rows[line : line + 1, : ref.shape[1]] = ref[...]
+        across = jnp.broadcast_to(key_rows[line : line + 1, :], (bs, bs))
+        return across, across.T
+
+    def newest(found, offset):
+        return jnp.max(jnp.where(found, first + (offset + 1), 0), axis=0, keepdims=True)
+
+    key_rows[...] = jnp.full(key_rows.shape, -1, jnp.int32)
+
+    def chain_of(line, main, live, more=None):
+        count = main.shape[1]
+        across, down = spread(main, 2 * line)
+        valid = first < live
+        prev_main = newest((across == down) & (first < second) & valid, 0)
+        ends = newest((second == down) & valid, 0)
+        if more is not None:
+            across_more, down_more = spread(more, 2 * line + 1)
+            known = first < more.shape[1]
+            prev_more = jnp.maximum(
+                newest((across_more == down) & valid, 0),
+                newest((across_more == down_more) & (first < second) & known, count),
+            )
+            ends = jnp.maximum(ends, newest((second == down_more) & known, count))
+            link_rows[3 * line + 1 : 3 * line + 2, :] = prev_more
+        link_rows[3 * line : 3 * line + 1, :] = prev_main
+        link_rows[3 * line + 2 : 3 * line + 3, :] = ends
+
+    link_rows[...] = jnp.zeros(link_rows.shape, jnp.int32)
+    chain_of(0, keys_f, tile_count[0])
+    chain_of(1, keys_b, tile_count[0], keys_bs)
+    chain_of(2, keys_m, keys_m.shape[1])
+    chain_of(3, keys_n, keys_n.shape[1], keys_ns)
+    chain_of(4, keys_t, keys_t.shape[1])
+    link_copy = pltpu.make_async_copy(link_rows, link, load_sem.at[len(loads)])
+    link_copy.start()
+
     def pool_block(j):
         index = fine_pool[pl.ds(j, 1), :]
         for i in range(m_blocks):
@@ -280,17 +370,23 @@
 
     loop(blocks, pool_block)
 
-    def pool_into(part, values):
-        def one(m):
-            part[m] = mm(pool_map[pl.ds(pl.multiple_of(m * chunk, chunk), chunk), :], values[...]).astype(
-                BF16
-            )
-
-        loop(n_col, one)
-
-    pool_into(part_g, cot)
-    slots_g[c] = part_g[c]
-    scatter_g.start()
+    def pooled(values, m):
+        rows_at = pl.ds(pl.multiple_of(m * chunk, chunk), chunk)
+        return mm(pool_map[rows_at, :], values[...]).astype(BF16)
+
+    def pool_and_send(exchange, part, values):
+        def one(p):
+            part[p] = pooled(values, p)
+
+        exchange.start(one)
+        exchange.slots[c] = pooled(values, c)
+
+    pool_and_send(scatter_g, part_g, cot)
+    for j in range(m_blocks):
+        ids = lax.broadcasted_iota(jnp.int32, (bs, bs), 0) + c * bs
+        top_map[:, j * bs : (j + 1) * bs] = jnp.where(
+            ids == middle_pool[j : j + 1, :], 1.0, 0.0
+        ).astype(BF16)
 
     def flip(k):
         bank_t[k] = bank[k].astype(F32).T.astype(BF16)
@@ -298,38 +394,33 @@
     loop(kinds, flip, 4)
     for item in halo:
         item.wait()
+    link_copy.wait()
     scatter_g.wait()
     full_g[c] = scatter_g.total().astype(BF16)
     gather_g.start()
 
     def fine_slot(t):
-        chain[t + 1] = mm(bank[fine_kind[t]], ext[fine_source[t]]) + chain[prev[0, t]]
+        chain[t + 1] = mm(bank[fine_kind[t]], ext[fine_source[t]]) + chain[link[0, t]]
 
     loop(fine_kind.shape[0], fine_slot, UNROLL)
 
     def fine_state(b):
         at = pl.ds(pl.multiple_of(b * bs, bs), bs)
-        value, rate = gelu_pair(chain[last[0, b]])
+        value, rate = gelu_pair(chain[link[2, b]])
         state = feat[at, :].astype(F32) + value
         hidden[at, :] = state
         slope[at, :] = rate
         grad_sum[at, :] = state.astype(BF16)
 
     loop(blocks, fine_state)
-    pool_into(part_h, grad_sum)
-    slots_h[c] = part_h[c]
-    scatter_h.start()
+    pool_and_send(scatter_h, part_h, grad_sum)
 
     gather_g.wait()
     for k in range(n_col):
         m_gsum[k * chunk : (k + 1) * chunk, :] = full_g[k].astype(F32) * p2
 
     def top_partial(values):
-        maps = []
-        for j in range(m_blocks):
-            ids = lax.broadcasted_iota(jnp.int32, (bs, bs), 0) + c * bs
-            maps.append(jnp.where(ids == middle_pool[j : j + 1, :], 1.0, 0.0).astype(BF16))
-        return mm(jnp.concatenate(maps, axis=1), values)
+        return mm(top_map[...], values)
 
     top_slots_g[r] = top_partial(m_gsum[...].astype(BF16)).astype(BF16)
     rows_g.start()
@@ -365,18 +456,27 @@
             m_send[k, i] = m_grad[middle_sends[k * m_send_n + i]]
     for item in m_halo:
         item.start()
+
+    def middle_map_block(j):
+        at = pl.ds(pl.multiple_of(j * bs, bs), bs)
+        index = jnp.broadcast_to(middle_pool[pl.ds(j, 1), :].astype(F32), (bs, bs)).T
+        for i in range(n_col):
+            ids = (lax.broadcasted_iota(jnp.int32, (bs, bs), 1) + i * bs).astype(F32)
+            middle_map[at, i * bs : (i + 1) * bs] = jnp.where(ids == index, 1.0, 0.0).astype(BF16)
+
+    loop(m_blocks, middle_map_block)
     cols_g.wait()
     for item in m_halo:
         item.wait()
 
     def middle_slot(t):
-        chain[t + 1] = mm(bank[middle_kind[t]], m_ext[middle_source[t]]) + chain[prev[2, t]]
+        chain[t + 1] = mm(bank[middle_kind[t]], m_ext[middle_source[t]]) + chain[link[6, t]]
 
     loop(middle_kind.shape[0], middle_slot, UNROLL)
 
     def middle_state(b):
         at = pl.ds(pl.multiple_of(b * bs, bs), bs)
-        value, rate = gelu_pair(chain[last[2, b]])
+        value, rate = gelu_pair(chain[link[8, b]])
         m_hidden[at, :] = m_hidden[at, :] + value
         m_slope[at, :] = rate
 
@@ -408,13 +508,13 @@
     def top_back(b):
         for s in range(t_slots):
             t = b * t_slots + s
-            chain[t + 1] = mm(bank_t[top_kind[t]], t_gsum[b]) + chain[prev[4, t]]
+            chain[t + 1] = mm(bank_t[top_kind[t]], t_gsum[b]) + chain[link[12, t]]
 
     loop(n_col, top_back)
 
     def top_grad(b):
         at = pl.ds(pl.multiple_of(b * bs, bs), bs)
-        message_grad = chain[last[4, b]].astype(BF16)
+        message_grad = chain[link[14, b]].astype(BF16)
         t_gmsg[at, :] = message_grad
         t_table[at, width:] = (
             top_g[b].astype(F32) + mm_nt(message_grad, w_top[...])
@@ -424,12 +524,7 @@
 
     def middle_pick(j):
         at = pl.ds(pl.multiple_of(j * bs, bs), bs)
-        index = jnp.broadcast_to(middle_pool[pl.ds(j, 1), :].astype(F32), (bs, bs)).T
-        maps = []
-        for i in range(n_col):
-            ids = (lax.broadcasted_iota(jnp.int32, (bs, bs), 1) + i * bs).astype(F32)
-            maps.append(jnp.where(ids == index, 1.0, 0.0).astype(BF16))
-        picked = mm(jnp.concatenate(maps, axis=1), t_table[...]) * p3
+        picked = mm(middle_map[at, :], t_table[...]) * p3
         table[at, :] = (m_hidden[at, :] + picked[:, :width]).astype(BF16)
         grad = m_gsum[at, :] + picked[:, width:]
         m_gsum[at, :] = grad
@@ -438,13 +533,13 @@
     loop(m_blocks, middle_pick)
 
     def middle_back(t):
-        chain[t + 1] = mm(bank_t[middle_kind[t]], m_grad[middle_target[t]]) + chain[prev[3, t]]
+        chain[t + 1] = mm(bank_t[middle_kind[t]], m_grad[middle_target[t]]) + chain[link[9, t]]
 
     m_count = middle_kind.shape[0]
     loop(m_count, middle_back, UNROLL)
     for k in range(2):
         for i in range(m_send_n):
-            m_back[k, i] = chain[last[3, m_blocks + k * m_send_n + i]].astype(BF16)
+            m_back[k, i] = chain[link[11, m_blocks + k * m_send_n + i]].astype(BF16)
     for item in m_homes:
         item.start()
 
@@ -461,12 +556,12 @@
         item.wait()
     for k in range(2):
         for i in range(m_send_n):
-            t = m_count + k * m_send_n + i
-            chain[t + 1] = m_home[k, i].astype(F32) + chain[prev[3, t]]
+            t = k * m_send_n + i
+            chain[m_count + t + 1] = m_home[k, i].astype(F32) + chain[link[10, t]]
 
     def middle_grad(b):
         at = pl.ds(pl.multiple_of(b * bs, bs), bs)
-        message_grad = chain[last[3, b]].astype(BF16)
+        message_grad = chain[link[11, b]].astype(BF16)
         m_gmsg[at, :] = message_grad
         table[at, :] = (m_gsum[at, :] + mm_nt(message_grad, w_middle[...])).astype(BF16)
 
@@ -486,12 +581,12 @@
     f_count = fine_kind.shape[0]
 
     def fine_back(t):
-        chain[t + 1] = mm(bank_t[fine_kind[t]], grad_blocks[fine_target[t]]) + chain[prev[1, t]]
+        chain[t + 1] = mm(bank_t[fine_kind[t]], grad_blocks[fine_target[t]]) + chain[link[3, t]]
 
     loop(f_count, fine_back, UNROLL)
     for k in range(4):
         for i in range(send):
-            back_fine[k, i] = chain[last[1, blocks + k * send + i]].astype(BF16)
+            back_fine[k, i] = chain[link[5, blocks + k * send + i]].astype(BF16)
     for item in home:
         item.start()
     sum_middle.wait()
@@ -500,12 +595,12 @@
         item.wait()
     for k in range(4):
         for i in range(send):
-            t = f_count + k * send + i
-            chain[t + 1] = home_fine[k, i].astype(F32) + chain[prev[1, t]]
+            t = k * send + i
+            chain[f_count + t + 1] = home_fine[k, i].astype(F32) + chain[link[4, t]]
 
     def fine_message_grad(b):
         at = pl.ds(pl.multiple_of(b * bs, bs), bs)
-        grad_sum[at, :] = chain[last[1, b]].astype(BF16)
+        grad_sum[at, :] = chain[link[5, b]].astype(BF16)
 
     loop(blocks, fine_message_grad)
     scale = (rows * n_row * n_col) ** (-0.5)
@@ -523,17 +618,6 @@
     loop(blocks // 2, lambda b: fine_final(b + blocks // 2))
     sum_fine_row.wait()
     weight_out[0] = sum_fine_row.total()
-
-
-def links(keys, live, extent):
-    pos = jnp.arange(keys.shape[1], dtype=jnp.int32)
-    valid = live[:, None, :]
-    same = (keys[:, :, None] == keys[:, None, :]) & (pos[None, None, :] < pos[None, :, None]) & valid
-    prev = jnp.max(jnp.where(same, pos + 1, 0), axis=2)
-    ids = jnp.arange(extent, dtype=jnp.int32)
-    ends = (keys[:, None, :] == ids[None, :, None]) & valid
-    last = jnp.max(jnp.where(ends, pos + 1, 0), axis=2)
-    return prev, last
 
 
 def local(
@@ -571,27 +655,6 @@
     chunk = m_rows // n_col
     f_count = fine_kind.shape[0]
     length = f_count + 4 * send
-    extent = max(blocks + 4 * send, m_blocks + 2 * m_send, n_col)
-
-    def padded(*pieces):
-        key = jnp.concatenate(pieces)
-        return jnp.pad(key, (0, length - key.shape[0]), constant_values=-1)
-
-    keys = jnp.stack(
-        [
-            padded(fine_target),
-            padded(fine_source, fine_sends),
-            padded(middle_target),
-            padded(middle_source, middle_sends),
-            padded(top_source),
-        ]
-    )
-    pos = jnp.arange(length, dtype=jnp.int32)
-    alive = (pos < tile_count[0]) | (pos >= f_count)
-    level = jnp.arange(5, dtype=jnp.int32)
-    live = alive[None, :] | (level[:, None] >= 2)
-    prev, last = links(keys, live, extent)
-
     def block_buf(*lead):
         return pltpu.VMEM(lead + (bs, width), BF16)
 
@@ -600,7 +663,28 @@
 
     part = pltpu.VMEM((n_col, chunk, width), BF16)
     n_sem = 12 + 8 * n_col + 4 * n_row
-    scratch = [
+    arrays = [
+        features,
+        cotangent,
+        fine_weight,
+        middle_weight,
+        top_weight,
+        tile_bank,
+        fine_pool.reshape(blocks, bs),
+        middle_pool.reshape(m_blocks, bs),
+    ] + [
+        key.reshape(1, key.shape[0])
+        for key in (
+            fine_target,
+            fine_source,
+            fine_sends,
+            middle_target,
+            middle_source,
+            middle_sends,
+            top_source,
+        )
+    ]
+    scratch = [pltpu.VMEM(array.shape, array.dtype) for array in arrays] + [
         block_buf(kinds),
         pltpu.VMEM((m_rows, rows), BF16),
         pltpu.VMEM((rows, m_rows), BF16),
@@ -637,12 +721,17 @@
         block_buf(n_col),
         block_buf(n_col),
         block_buf(n_col),
-        pltpu.VMEM((8, width), F32),
         wide_buf(n_col * bs, BF16),
         pltpu.VMEM((n_col * bs, 2 * width), BF16),
         block_buf(n_row),
         block_buf(n_col),
         block_buf(n_row),
+        pltpu.VMEM((bs, m_rows), BF16),
+        pltpu.VMEM((m_rows, n_col * bs), BF16),
+        pltpu.VMEM((16, bs), jnp.int32),
+        pltpu.VMEM((16, bs), jnp.int32),
+        pltpu.SMEM((16, bs), jnp.int32),
+        pltpu.SemaphoreType.DMA((len(arrays) + 1,)),
         pltpu.SemaphoreType.DMA((n_sem,)),
         pltpu.SemaphoreType.DMA((n_sem,)),
     ]
@@ -655,18 +744,17 @@
             jax.ShapeDtypeStruct((rows, width), BF16),
             jax.ShapeDtypeStruct((3, width, width), F32),
         ),
-        in_specs=[smem] * 12 + [vmem] * 8,
+        in_specs=[smem] * 11 + [pl.BlockSpec(memory_space=pl.ANY)] * len(arrays),
         out_specs=(vmem, vmem, vmem),
         scratch_shapes=scratch,
         compiler_params=pltpu.CompilerParams(
-            collective_id=0, has_side_effects=True, vmem_limit_bytes=48 * 1024 * 1024
+            collective_id=0, has_side_effects=True, vmem_limit_bytes=56 * 1024 * 1024
         ),
         cost_estimate=pl.CostEstimate(
             flops=4_000_000_000, bytes_accessed=4_000_000, transcendentals=400_000
         ),
     )(
-        prev,
-        last,
+        tile_count,
         fine_source,
         fine_target,
         fine_kind,
@@ -677,14 +765,7 @@
         middle_sends,
         top_source,
         top_kind,
-        features,
-        cotangent,
-        fine_weight,
-        middle_weight,
-        top_weight,
-        tile_bank,
-        fine_pool.reshape(blocks, bs),
-        middle_pool.reshape(m_blocks, bs),
+        *arrays,
     )
 
 

time: 82.1 us -> 74 us (0.901)
  local copies, waits for them, and re-layouts: 9.21 us -> 3.72 us
  Pallas kernels: 70.3 us -> 68.8 us
    unnamed x39 -> x7, local copies, waits for them, and re-layouts: 9.17 us -> 3.72 us
    pallas_call x1, Pallas kernels: 70.3 us -> 68.8 us  [local(): pl.pallas_call(functools.partial(kernel, (n_row, n_col, send, m_send, t_s...]
where the time goes in v2:
time: 74 us; the launch traced here: 73.8 us
  Pallas kernels  68.8 us (93%)
  local copies, waits for them, and re-layouts  3.72 us (5%)
  between operations  1.3 us (2%)
    pallas_call x1, Pallas kernels, local(): pl.pallas_call(functools.partial(kernel, (n_row, n_col, send, m_send, t_s...  68.8 us
    unnamed x7, local copies, waits for them, and re-layouts  3.72 us

profile of v2, /device:TPU:0, one launch (start us, length us, event | category | flops | bytes accessed | tf_op | source)
XLA Modules:
  0.0 73.8 jit_solution(14964043889045424714)
XLA Ops:
  1.3 68.8 %shard_map.202 = (bf16[2048,128]{1,0:T(8,128)(2,1)}, bf16[2048,128]{1,0:T(8,128)(2,1)}, f32[3,128,128]{2,1,0:T(8,128)}) custom-call(s32[1]{0:T(128)S(6)} %copy.25.tile_count, s32[128]{0:T(128)} %fine_source.1, s32[128]{0:T(128)} %fine_target.1, s32[128]{0:T(128)} %fine_kind.1, s32[8]{0:T(128)} %fine_sends.1, s32[32]{0:T(128)} %middle_source.1, ...), custom_call_target="tpu_custom_call" | custom-call | flops 4000000000 | bytes 4000000 | tf_op jit(solution)/shard_map/pallas_call | solution.py:740
  70.1 0.0 copy-start
  70.1 1.9 %copy.26 = bf16[2048,128]{1,0:T(8,128)(2,1)} copy(bf16[2048,128]{1,0:T(8,128)(2,1)} %get-tuple-element.6) | data formatting | bytes 1048576
  72.0 0.0 copy-done
  72.0 0.0 copy-start.1
  72.0 0.8 %copy.27 = bf16[2048,128]{1,0:T(8,128)(2,1)} copy(bf16[2048,128]{1,0:T(8,128)(2,1)S(1)} %copy-done) | data formatting | bytes 1048576
  72.8 0.3 copy-done.1
  73.1 0.7 copy.28
Async XLA Ops:
  70.1 1.9 %copy-start = (bf16[2048,128]{1,0:T(8,128)(2,1)S(1)}, bf16[2048,128]{1,0:T(8,128)(2,1)}, u32[]{:S(2)}) copy-start(bf16[2048,128]{1,0:T(8,128)(2,1)} %get-tuple-element.7) | copy-start | bytes 1572868
  72.0 1.1 %copy-start.1 = (f32[3,128,128]{2,1,0:T(8,128)S(1)}, f32[3,128,128]{2,1,0:T(8,128)}, u32[]{:S(2)}) copy-start(f32[3,128,128]{2,1,0:T(8,128)} %get-tuple-element.8) | copy-start | bytes 589828

commit v3 on v2

--- a/solution.py
+++ b/solution.py
@@ -388,28 +388,26 @@
             ids == middle_pool[j : j + 1, :], 1.0, 0.0
         ).astype(BF16)
 
-    def flip(k):
-        bank_t[k] = bank[k].astype(F32).T.astype(BF16)
-
-    loop(kinds, flip, 4)
     for item in halo:
         item.wait()
     link_copy.wait()
+
+    def fine_slot(t):
+        chain[t + 1] = mm(bank[fine_kind[t]], ext[fine_source[t]]) + chain[link[0, t]]
+
+    half = fine_kind.shape[0] // 2
+    loop(half, fine_slot, UNROLL)
     scatter_g.wait()
     full_g[c] = scatter_g.total().astype(BF16)
     gather_g.start()
-
-    def fine_slot(t):
-        chain[t + 1] = mm(bank[fine_kind[t]], ext[fine_source[t]]) + chain[link[0, t]]
-
-    loop(fine_kind.shape[0], fine_slot, UNROLL)
+    loop(half, lambda t: fine_slot(t + half), UNROLL)
 
     def fine_state(b):
         at = pl.ds(pl.multiple_of(b * bs, bs), bs)
-        value, rate = gelu_pair(chain[link[2, b]])
-        state = feat[at, :].astype(F32) + value
+        total = chain[link[2, b]]
+        state = feat[at, :].astype(F32) + gelu_pair(total)[0]
         hidden[at, :] = state
-        slope[at, :] = rate
+        slope[at, :] = total
         grad_sum[at, :] = state.astype(BF16)
 
     loop(blocks, fine_state)
@@ -483,9 +481,20 @@
     loop(m_blocks, middle_state)
     top_slots_h[r] = top_partial(m_hidden[...].astype(BF16)).astype(BF16)
     rows_h.start()
+
+    def flip(k):
+        bank_t[k] = bank[k].astype(F32).T.astype(BF16)
+
+    loop(kinds, flip, 4)
     rows_h.wait()
     top_h[c] = (rows_h.total() * p3).astype(BF16)
     cols_h.start()
+
+    def fine_slope(b):
+        at = pl.ds(pl.multiple_of(b * bs, bs), bs)
+        slope[at, :] = gelu_pair(slope[at, :])[1]
+
+    loop(blocks, fine_slope)
     cols_h.wait()
 
     def top_message(b):
@@ -748,7 +757,7 @@
         out_specs=(vmem, vmem, vmem),
         scratch_shapes=scratch,
         compiler_params=pltpu.CompilerParams(
-            collective_id=0, has_side_effects=True, vmem_limit_bytes=56 * 1024 * 1024
+            collective_id=0, has_side_effects=True, vmem_limit_bytes=48 * 1024 * 1024
         ),
         cost_estimate=pl.CostEstimate(
             flops=4_000_000_000, bytes_accessed=4_000_000, transcendentals=400_000

time: 74 us -> 76 us (1.027)
  local copies, waits for them, and re-layouts: 3.72 us -> 8.57 us
  Pallas kernels: 68.8 us -> 65.5 us
    unnamed x7 -> x39, local copies, waits for them, and re-layouts: 3.72 us -> 8.57 us
    pallas_call x1, Pallas kernels: 68.8 us -> 65.5 us  [local(): pl.pallas_call(functools.partial(kernel, (n_row, n_col, send, m_send, t_s...]
where the time goes in v3:
time: 76 us; the launch traced here: 75.5 us
  Pallas kernels  65.5 us (86%)
  local copies, waits for them, and re-layouts  8.57 us (11%)
  between operations  1.4 us (2%)
    pallas_call x1, Pallas kernels, local(): pl.pallas_call(functools.partial(kernel, (n_row, n_col, send, m_send, t_s...  65.5 us
    unnamed x39, local copies, waits for them, and re-layouts  8.57 us

profile of v3, /device:TPU:0, one launch (start us, length us, event | category | flops | bytes accessed | tf_op | source)
XLA Modules:
  0.0 75.5 jit_solution(16121977965790684890)
XLA Ops:
  1.3 0.0 copy-start.14
  1.3 0.0 copy-start.15
  1.3 0.0 copy-start.16
  1.3 0.0 copy-start.17
  1.3 0.0 copy-start.6
  1.3 0.0 copy-start.7
  1.3 0.0 copy-start.11
  1.4 0.0 copy-start.12
  1.4 0.0 copy-start.13
  1.4 0.0 copy-start.8
  1.4 0.0 copy-start.9
  1.4 0.0 copy-start.10
  1.4 0.5 copy-done.14
  1.9 0.0 copy-done.15
  2.0 0.0 copy-done.16
  2.0 0.0 copy-done.17
  2.0 0.1 copy-done.6
  2.0 0.0 copy-done.7
  2.1 0.0 copy-done.13
  2.1 0.0 copy-done.8
  2.1 0.0 copy-done.9
  2.1 0.0 copy-done.10
  2.1 1.2 %copy-done = bf16[32,128,128]{2,1,0:T(8,128)(2,1)S(1)} copy-done((bf16[32,128,128]{2,1,0:T(8,128)(2,1)S(1)}, bf16[32,128,128]{2,1,0:T(8,128)(2,1)}, u32[]{:S(2)}) %copy-start) | copy-done | bytes 1048600
  3.3 1.0 %copy-done.1 = bf16[2048,128]{1,0:T(8,128)(2,1)S(1)} copy-done((bf16[2048,128]{1,0:T(8,128)(2,1)S(1)}, bf16[2048,128]{1,0:T(8,128)(2,1)}, u32[]{:S(2)}) %copy-start.1) | copy-done | bytes 524312
  4.4 1.0 %copy-done.2 = bf16[2048,128]{1,0:T(8,128)(2,1)S(1)} copy-done((bf16[2048,128]{1,0:T(8,128)(2,1)S(1)}, bf16[2048,128]{1,0:T(8,128)(2,1)}, u32[]{:S(2)}) %copy-start.2) | copy-done | bytes 524312
  5.4 0.8 %copy-done.3 = bf16[128,128]{1,0:T(8,128)(2,1)S(1)} copy-done((bf16[128,128]{1,0:T(8,128)(2,1)S(1)}, bf16[128,128]{1,0:T(8,128)(2,1)}, u32[]{:S(2)}) %copy-start.3) | copy-done | bytes 32792
  6.2 0.8 %copy-done.4 = bf16[128,128]{1,0:T(8,128)(2,1)S(1)} copy-done((bf16[128,128]{1,0:T(8,128)(2,1)S(1)}, bf16[128,128]{1,0:T(8,128)(2,1)}, u32[]{:S(2)}) %copy-start.4) | copy-done | bytes 32792
  6.9 0.8 %copy-done.5 = bf16[128,128]{1,0:T(8,128)(2,1)S(1)} copy-done((bf16[128,128]{1,0:T(8,128)(2,1)S(1)}, bf16[128,128]{1,0:T(8,128)(2,1)}, u32[]{:S(2)}) %copy-start.5) | copy-done | bytes 32792
  7.7 65.5 %shard_map.202 = (bf16[2048,128]{1,0:T(8,128)(2,1)S(1)}, bf16[2048,128]{1,0:T(8,128)(2,1)S(1)}, f32[3,128,128]{2,1,0:T(8,128)S(1)}) custom-call(s32[1]{0:T(128)S(6)} %copy.25.tile_count, s32[128]{0:T(128)S(1)} %copy-done.8, s32[128]{0:T(128)S(1)} %copy-done.9, s32[128]{0:T(128)S(1)} %copy-done.10, s32[8]{0:T(128)S(1)} %copy-done.11, s32[32]{0:T(128)S(1)} %copy-done.12, ...), custom_call_target="tpu_custom_call" | custom-call | flops 4000000000 | bytes 4000000 | tf_op jit(solution)/shard_map/pallas_call | solution.py:749
  73.2 0.8 %copy.26 = bf16[2048,128]{1,0:T(8,128)(2,1)} copy(bf16[2048,128]{1,0:T(8,128)(2,1)S(1)} %get-tuple-element.6) | data formatting | bytes 1048576
  74.0 0.8 %copy.27 = bf16[2048,128]{1,0:T(8,128)(2,1)} copy(bf16[2048,128]{1,0:T(8,128)(2,1)S(1)} %get-tuple-element.7) | data formatting | bytes 1048576
  74.8 0.7 copy.28
  (8 shorter events, 0.0 us)
Async XLA Ops:
  1.3 0.7 copy-start.14
  1.3 0.7 copy-start.15
  1.3 0.7 copy-start.16
  1.3 0.7 copy-start.17
  1.3 0.7 copy-start.6
  1.3 0.7 copy-start.7
  1.3 0.7 copy-start.11
  1.4 0.7 copy-start.12
  1.4 0.7 copy-start.13
  1.4 0.7 copy-start.8
  1.4 0.7 copy-start.9
  1.4 0.7 copy-start.10
  2.1 1.2 %copy-start = (bf16[32,128,128]{2,1,0:T(8,128)(2,1)S(1)}, bf16[32,128,128]{2,1,0:T(8,128)(2,1)}, u32[]{:S(2)}) copy-start(bf16[32,128,128]{2,1,0:T(8,128)(2,1)} %refs_5_.1) | copy-start | bytes 3145732
  3.3 1.0 %copy-start.1 = (bf16[2048,128]{1,0:T(8,128)(2,1)S(1)}, bf16[2048,128]{1,0:T(8,128)(2,1)}, u32[]{:S(2)}) copy-start(bf16[2048,128]{1,0:T(8,128)(2,1)} %refs_0_.1) | copy-start | bytes 1572868
  4.4 1.0 %copy-start.2 = (bf16[2048,128]{1,0:T(8,128)(2,1)S(1)}, bf16[2048,128]{1,0:T(8,128)(2,1)}, u32[]{:S(2)}) copy-start(bf16[2048,128]{1,0:T(8,128)(2,1)} %refs_1_.1) | copy-start | bytes 1572868
  5.4 0.8 %copy-start.3 = (bf16[128,128]{1,0:T(8,128)(2,1)S(1)}, bf16[128,128]{1,0:T(8,128)(2,1)}, u32[]{:S(2)}) copy-start(bf16[128,128]{1,0:T(8,128)(2,1)} %refs_2_.1) | copy-start | bytes 98308
  6.2 0.8 %copy-start.4 = (bf16[128,128]{1,0:T(8,128)(2,1)S(1)}, bf16[128,128]{1,0:T(8,128)(2,1)}, u32[]{:S(2)}) copy-start(bf16[128,128]{1,0:T(8,128)(2,1)} %refs_3_.1) | copy-start | bytes 98308
  6.9 0.8 %copy-start.5 = (bf16[128,128]{1,0:T(8,128)(2,1)S(1)}, bf16[128,128]{1,0:T(8,128)(2,1)}, u32[]{:S(2)}) copy-start(bf16[128,128]{1,0:T(8,128)(2,1)} %refs_4_.1) | copy-start | bytes 98308

commit v4 on v3

--- a/solution.py
+++ b/solution.py
@@ -629,6 +629,16 @@
     weight_out[0] = sum_fine_row.total()
 
 
+def write_out(*refs):
+    copies = [
+        pltpu.make_async_copy(refs[k], refs[3 + k], refs[6].at[k]) for k in range(3)
+    ]
+    for copy in copies:
+        copy.start()
+    for copy in copies:
+        copy.wait()
+
+
 def local(
     features,
     cotangent,
@@ -746,14 +756,14 @@
     ]
     smem = pl.BlockSpec(memory_space=pltpu.SMEM)
     vmem = pl.BlockSpec(memory_space=pltpu.VMEM)
-    return pl.pallas_call(
+    results = pl.pallas_call(
         functools.partial(kernel, (n_row, n_col, send, m_send, t_slots)),
         out_shape=(
             jax.ShapeDtypeStruct((rows, width), BF16),
             jax.ShapeDtypeStruct((rows, width), BF16),
             jax.ShapeDtypeStruct((3, width, width), F32),
         ),
-        in_specs=[smem] * 11 + [pl.BlockSpec(memory_space=pl.ANY)] * len(arrays),
+        in_specs=[smem] * 11 + [pl.BlockSpec(memory_space=pltpu.HBM)] * len(arrays),
         out_specs=(vmem, vmem, vmem),
         scratch_shapes=scratch,
         compiler_params=pltpu.CompilerParams(
@@ -776,6 +786,13 @@
         top_kind,
         *arrays,
     )
+    return pl.pallas_call(
+        write_out,
+        out_shape=[jax.ShapeDtypeStruct(x.shape, x.dtype) for x in results],
+        in_specs=[pl.BlockSpec(memory_space=pl.ANY)] * 3,
+        out_specs=[pl.BlockSpec(memory_space=pltpu.HBM)] * 3,
+        scratch_shapes=[pltpu.SemaphoreType.DMA((3,))],
+    )(*results)
 
 
 def solution(mesh):

time: 76 us -> 115 us (1.51)
  Pallas kernels: 65.5 us -> 104 us
    pallas_call x0 -> x1, Pallas kernels: none -> 38.8 us  [local(): pl.pallas_call(write_out, out_shape=[jax.ShapeDtypeStruct(x.shape, x.dtyp...]
    unnamed x39 -> x42, local copies, waits for them, and re-layouts: 8.57 us -> 8.57 us
where the time goes in v4:
time: 115 us; the launch traced here: 114 us
  Pallas kernels  104 us (90%)
  local copies, waits for them, and re-layouts  8.57 us (7%)
  between operations  1.41 us (1%)
    pallas_call x1, Pallas kernels, local(): pl.pallas_call(functools.partial(kernel, (n_row, n_col, send, m_send, t_s...  65.5 us
    pallas_call x1, Pallas kernels, local(): pl.pallas_call(write_out, out_shape=[jax.ShapeDtypeStruct(x.shape, x.dtyp...  38.8 us
    unnamed x42, local copies, waits for them, and re-layouts  8.57 us

profile of v4, /device:TPU:0, one launch (start us, length us, event | category | flops | bytes accessed | tf_op | source)
XLA Modules:
  0.0 114.3 jit_solution(13260759577715310579)
XLA Ops:
  1.3 0.0 copy-start.17
  1.3 0.0 copy-start.18
  1.3 0.0 copy-start.19
  1.3 0.0 copy-start.20
  1.3 0.0 copy-start.9
  1.3 0.0 copy-start.10
  1.3 0.0 copy-start.14
  1.4 0.0 copy-start.15
  1.4 0.0 copy-start.16
  1.4 0.0 copy-start.11
  1.4 0.0 copy-start.12
  1.4 0.5 copy-done.17
  1.9 0.0 copy-done.18
  2.0 0.0 copy-done.19
  2.0 0.0 copy-done.20
  2.0 0.1 copy-done.9
  2.0 0.0 copy-done.10
  2.1 0.0 copy-done.16
  2.1 0.0 copy-done.11
  2.1 0.0 copy-done.12
  2.1 0.0 copy-done.13
  2.1 1.2 %copy-done.3 = bf16[32,128,128]{2,1,0:T(8,128)(2,1)S(1)} copy-done((bf16[32,128,128]{2,1,0:T(8,128)(2,1)S(1)}, bf16[32,128,128]{2,1,0:T(8,128)(2,1)}, u32[]{:S(2)}) %copy-start.3) | copy-done | bytes 1048600
  3.3 1.0 copy-done.4
  4.4 1.0 copy-done.5
  5.4 0.8 copy-done.6
  6.2 0.8 copy-done.7
  6.9 0.8 copy-done.8
  7.7 65.5 %shard_map.202 = (bf16[2048,128]{1,0:T(8,128)(2,1)S(1)}, bf16[2048,128]{1,0:T(8,128)(2,1)S(1)}, f32[3,128,128]{2,1,0:T(8,128)S(1)}) custom-call(s32[1]{0:T(128)S(6)} %copy.22.tile_count, s32[128]{0:T(128)S(1)} %copy-done.11, s32[128]{0:T(128)S(1)} %copy-done.12, s32[128]{0:T(128)S(1)} %copy-done.13, s32[8]{0:T(128)S(1)} %copy-done.14, s32[32]{0:T(128)S(1)} %copy-done.15, ...), custom_call_target="tpu_custom_call" | custom-call | flops 4000000000 | bytes 4000000 | tf_op jit(solution)/shard_map/pallas_call | solution.py:759
  73.2 0.8 copy-done
  74.0 0.8 copy-done.1
  74.8 0.7 copy-done.2
  75.5 38.8 %shard_map.203 = (bf16[2048,128]{1,0:T(8,128)(2,1)}, bf16[2048,128]{1,0:T(8,128)(2,1)}, f32[3,128,128]{2,1,0:T(8,128)}) custom-call(bf16[2048,128]{1,0:T(8,128)(2,1)} %copy-done, bf16[2048,128]{1,0:T(8,128)(2,1)} %copy-done.1, f32[3,128,128]{2,1,0:T(8,128)} %copy-done.2), custom_call_target="tpu_custom_call" | custom-call | tf_op jit(solution)/shard_map/pallas_call | solution.py:789
  (12 shorter events, 0.0 us)
Async XLA Ops:
  1.3 0.7 copy-start.17
  1.3 0.7 copy-start.18
  1.3 0.7 copy-start.19
  1.3 0.7 copy-start.20
  1.3 0.7 copy-start.9
  1.3 0.7 copy-start.10
  1.3 0.7 copy-start.14
  1.4 0.7 copy-start.15
  1.4 0.7 copy-start.16
  1.4 0.7 copy-start.11
  1.4 0.7 copy-start.12
  1.4 0.7 copy-start.13
  2.1 1.2 %copy-start.3 = (bf16[32,128,128]{2,1,0:T(8,128)(2,1)S(1)}, bf16[32,128,128]{2,1,0:T(8,128)(2,1)}, u32[]{:S(2)}) copy-start(bf16[32,128,128]{2,1,0:T(8,128)(2,1)} %refs_5_.1) | copy-start | bytes 3145732
  3.3 1.0 copy-start.4
  4.4 1.0 copy-start.5
  5.4 0.8 copy-start.6
  6.2 0.8 copy-start.7
  6.9 0.8 copy-start.8
  73.2 0.8 copy-start
  74.0 0.8 copy-start.1
  74.8 0.7 copy-start.2
